TPU v7x, 1024 devices: a whole 4x4x32 slice. The times are simulated.
1024 devices in a mesh: task: 32 (over z_hi, y, x), integ: 32 (over z_lo, core).
Axes of the slice: x: 4, y: 4, z: 32 (z_hi: 2, z_lo: 16; z = z_hi * 16 + z_lo), core: 2. Of those that a mesh axis runs over, the one named last changes fastest.
Arguments:
- amplitudes: bfloat16 [4096, 98304], P('integ', 'task'), may hold values from -6 to 6
- integrals: bfloat16 [98304, 1024], P(('task', 'integ')), may hold values from -0.0546875 to 0.0546875
- block_mask: int32 [768, 8], replicated, may hold values from 0 to 1, as said below
- residual_in: float32 [4096, 1024], P(('integ', 'task')), may hold values from -6 to 6
Outputs:
- residual_out: float32 [4096, 1024], P(('integ', 'task'))
Inputs may be any that keep to these rules, and one draw needn't show every extreme that they name: block_mask[k, b] is 1 exactly when block k and block b carry the same one of 8 symmetry labels; every label carried by a residual block is carried by exactly 2 residual blocks, so a row of block_mask holds 0 or 2 ones.
All inputs are finite; a program needn't handle non-finite values.
Results may differ from a plain program's by a relative error of at most 0.0003.
Values may be sent and summed in bfloat16 or wider, within the bound.
No kernel may reach another device: no remote copies, remote signals or barrier semaphores. Data moves between devices by JAX's collectives and lax.ppermute only.
A program may use at most 32 MiB of HBM per device.

v0:
```python
import jax
import jax.numpy as jnp
from jax import lax
from jax.sharding import PartitionSpec as P

TILE = 128


def per_device(amplitudes, integrals, block_mask, residual_in):
    task_id = lax.axis_index("task")
    integ_id = lax.axis_index("integ")
    n_integ = lax.axis_size("integ")
    local_rows = integrals.shape[0]
    cd_tiles = block_mask.shape[0]
    row_start = (task_id * n_integ + integ_id) * local_rows
    row_tile = (row_start + jnp.arange(local_rows)) // TILE
    onehot = (row_tile[:, None] == jnp.arange(cd_tiles)[None, :]).astype(jnp.float32)
    row_mask = jnp.dot(onehot, block_mask.astype(jnp.float32))
    col_mask = jnp.repeat(row_mask, TILE, axis=1)
    masked = (integrals.astype(jnp.float32) * col_mask).astype(jnp.bfloat16)
    ladder = jnp.dot(
        amplitudes,
        lax.all_gather(masked, "integ", axis=0, tiled=True),
        preferred_element_type=jnp.float32,
    )
    summed = lax.psum_scatter(0.5 * ladder, "task", scatter_dimension=0, tiled=True)
    return residual_in + summed


def solution(mesh):
    return jax.shard_map(
        per_device,
        mesh=mesh,
        in_specs=(P("integ", "task"), P(("task", "integ"), None), P(), P(("integ", "task"), None)),
        out_specs=P(("integ", "task"), None),
        check_vma=False,
    )
```

profile of v0, /device:TPU:1, one launch (start us, length us, event | category | flops | bytes accessed | tf_op | source)
XLA Modules:
  0.0 1222.0 jit_solution(12188444088095724437)
XLA Ops:
  6.5 0.0 copy-start
  6.5 0.0 copy-start.1
  6.5 0.0 all-gather.2.cloned.1.call-start
  6.6 1.0 fusion.2
  7.6 0.2 broadcast_in_dim.2
  7.8 1.7 fusion.1
  9.5 0.0 all-gather.2.cloned.1.call-update
  9.5 0.0 all-reduce.3.cloned.1.call-start
  9.5 344.4 %all-gather.2.cloned.1.call-done = bf16[3072,1024]{1,0:T(8,128)(2,1)} async-done(((bf16[96,1024]{1,0:T(8,128)(2,1)}), bf16[3072,1024]{1,0:T(8,128)(2,1)}) %all-gather.2.cloned.1.call-update) | async-done | bytes 6291472 | tf_op jit(solution)/shard_map/all_gather | solution.py:23
  353.9 0.0 copy-done
  353.9 5.4 fusion
  359.3 0.0 all-reduce.3.cloned.1.call-update
  359.4 1.3 dynamic-slice
  361.3 851.8 %all-reduce.3.cloned.1.call-done = f32[128,1024]{0,1:T(8,128)} async-done(((f32[128,1024]{0,1:T(8,128)}), f32[128,1024]{0,1:T(8,128)}) %all-reduce.3.cloned.1.call-update) | async-done | bytes 524304
  1213.1 1.2 constant_dynamic-slice_fusion
  1214.3 0.2 copy.12
  1214.5 0.0 copy-done.1
  1214.5 0.6 add.26
  (1 shorter events, 0.0 us)
Async XLA Ops:
  6.5 347.4 %copy-start = (bf16[128,3072]{1,0:T(8,128)(2,1)S(1)}, bf16[128,3072]{1,0:T(8,128)(2,1)}, u32[]{:S(2)}) copy-start(bf16[128,3072]{1,0:T(8,128)(2,1)} %param.4) | copy-start | bytes 2359300
  6.5 1208.0 %copy-start.1 = (f32[4,1024]{1,0:T(4,128)S(1)}, f32[4,1024]{1,0:T(4,128)}, u32[]{:S(2)}) copy-start(f32[4,1024]{1,0:T(4,128)} %param.7) | copy-start | bytes 49156
  6.5 347.4 %all-gather.2.cloned.1.call-start = ((), (), s32[]{:S(2)}) async-start(), calls=%async_computation | async-start | bytes 6488064 | tf_op jit(solution)/shard_map/all_gather | solution.py:23
  9.5 1203.6 %all-reduce.3.cloned.1.call-start = ((), (), s32[]{:S(2)}) async-start(), calls=%async_computation.1 | async-start | bytes 1048576
Sparse Core Ops, SparseCore 0:
  10.0 343.8 all-gather.1
  359.5 853.5 all-reduce.2
where the time goes:
time: 1240 us; the launch traced here: 1220 us
  waiting for transfers between devices  1200 us (97%)
  between operations  14.1 us (1%)
    unnamed x3, waiting for transfers between devices  852 us
    all_gather x1, waiting for transfers between devices, per_device(): lax.all_gather(masked, 'integ', axis=0, tiled=True)  344 us
  transfers between devices with their start and end apart: 2, of which 2 were waited for; matrix products, arithmetic and copies ran while one was open for 0% of the time, Pallas kernels for 0%

commit v1 on v0

v1 whole, which is shorter than its diff:
```python
import jax
import jax.numpy as jnp
from jax import lax
from jax.experimental import pallas as pl
from jax.experimental.pallas import tpu as pltpu
from jax.sharding import Mesh
from jax.sharding import PartitionSpec as P

TILE = 128
ROWS = 96
GROUP = 32
TASK = ("zh", "y", "x")
INTEG = ("z8", "z4", "z2", "z1", "c")
SIZES = (2, 4, 4, 2, 2, 2, 2, 2)
GATHERS = ("z8", "z4", ("z2", "z1"))
SWAP = ((0, 1), (1, 0))


def chip_of(slot):
    z2, z1, z4, z8 = (slot >> 3) & 1, (slot >> 2) & 1, (slot >> 1) & 1, slot & 1
    return z8 * 8 + z4 * 4 + z2 * 2 + z1


def blocks_of(mask, tile):
    first, second, count = jnp.int32(0), jnp.int32(0), jnp.int32(0)
    for b in range(8):
        one = mask[tile, b] != 0
        first = jnp.where(one & (count == 0), b, first)
        second = jnp.where(one & (count == 1), b, second)
        count = count + one.astype(jnp.int32)
    return first, second, count


def block_cols(block):
    return pl.ds(pl.multiple_of(block * TILE, TILE), TILE)


def fetch_mask(mask_hbm, mask, sem):
    tiles = mask.shape[0]
    task = lax.axis_index(TASK)
    copy = pltpu.make_async_copy(mask_hbm.at[pl.ds(pl.multiple_of(task * tiles, 8), tiles)], mask, sem)
    copy.start()
    copy.wait()


def compress_kernel(mask_hbm, rows_ref, out_ref, mask, sem):
    fetch_mask(mask_hbm, mask, sem)
    integ = lax.axis_index(INTEG)
    for g in range(ROWS // GROUP):
        tile = (integ * ROWS + g * GROUP) // TILE
        first, second, count = blocks_of(mask, tile)
        rows = pl.ds(g * GROUP, GROUP)
        for half, block in ((0, first), (1, second)):
            part = rows_ref[rows, block_cols(block)]
            out_ref[rows, pl.ds(half * TILE, TILE)] = jnp.where(count > half, part, jnp.zeros_like(part))


def ladder_kernel(mask_hbm, amp_ref, own_ref, other_ref, out_ref, mask, packed, total, sem):
    fetch_mask(mask_hbm, mask, sem)
    core = lax.axis_index("c")
    for slot in range(16):
        rows = pl.ds(slot * ROWS, ROWS)
        for which, ref in ((core, own_ref), (1 - core, other_ref)):
            at = pl.multiple_of((2 * chip_of(slot) + which) * ROWS, GROUP)
            packed[pl.ds(at, ROWS), :] = ref[rows, :]
    total[...] = jnp.zeros_like(total)
    for tile in range(mask.shape[0]):
        first, second, _ = blocks_of(mask, tile)
        cols = pl.ds(tile * TILE, TILE)
        part = jnp.dot(amp_ref[:, cols], packed[cols, :], preferred_element_type=jnp.float32)
        total[:, block_cols(first)] += part[:, :TILE]
        total[:, block_cols(second)] += part[:, TILE:]
    largest = jnp.max(jnp.abs(total[...]))
    exponent = jnp.floor(jnp.log2(jnp.maximum(jnp.full((8, TILE), largest), 2.0**-100))) - 10.0
    width = total.shape[1]
    out_ref[:, :width] = (total[...] * (0.5 * jnp.exp2(-exponent[:1, :1]))).astype(out_ref.dtype)
    out_ref[:, width:] = jnp.broadcast_to(exponent[:1], (total.shape[0], TILE)).astype(out_ref.dtype)


def combine_kernel(parts_ref, residual_ref, out_ref):
    width = out_ref.shape[1]
    total = residual_ref[...]
    for task in range(parts_ref.shape[0]):
        scale = jnp.exp2(parts_ref[task, :, width:].astype(jnp.float32))
        total = total + parts_ref[task, :, :width].astype(jnp.float32) * scale[:, :1]
    out_ref[...] = total


def per_device(amplitudes, integrals, block_mask, residual_in):
    cd_tiles, ab_tiles = block_mask.shape
    pairs, width = amplitudes.shape[0], ab_tiles * TILE
    tasks = lax.axis_size(TASK)
    tiles = cd_tiles // tasks
    any_spec = pl.BlockSpec(memory_space=pl.ANY)
    vmem_spec = pl.BlockSpec(memory_space=pltpu.VMEM)
    packed = pl.pallas_call(
        compress_kernel,
        out_shape=jax.ShapeDtypeStruct((ROWS, 2 * TILE), jnp.bfloat16),
        in_specs=[any_spec, vmem_spec],
        out_specs=vmem_spec,
        scratch_shapes=[pltpu.SMEM((tiles, ab_tiles), jnp.int32), pltpu.SemaphoreType.DMA],
        name="compress",
    )(block_mask, integrals)
    for axis in GATHERS:
        packed = lax.all_gather(packed, axis, axis=0, tiled=True)
    other = lax.ppermute(packed, "c", SWAP)
    ladder = pl.pallas_call(
        ladder_kernel,
        out_shape=jax.ShapeDtypeStruct((pairs, width + TILE), jnp.float32),
        in_specs=[any_spec] + [vmem_spec] * 3,
        out_specs=vmem_spec,
        scratch_shapes=[
            pltpu.SMEM((tiles, ab_tiles), jnp.int32),
            pltpu.VMEM((32 * ROWS, 2 * TILE), jnp.bfloat16),
            pltpu.VMEM((pairs, width), jnp.float32),
            pltpu.SemaphoreType.DMA,
        ],
        compiler_params=pltpu.CompilerParams(vmem_limit_bytes=32 * 1024 * 1024),
        name="ladder",
    )(block_mask, amplitudes, packed, other)
    messages = ladder.astype(jnp.float16).reshape(tasks, pairs // tasks, width + TILE)
    parts = lax.all_to_all(messages, TASK, 0, 0, tiled=True).astype(jnp.float32)
    return pl.pallas_call(
        combine_kernel,
        out_shape=jax.ShapeDtypeStruct(residual_in.shape, jnp.float32),
        in_specs=[vmem_spec] * 2,
        out_specs=vmem_spec,
        name="combine",
    )(parts, residual_in)


def solution(mesh):
    fine = Mesh(mesh.devices.reshape(SIZES), TASK + INTEG)
    return jax.shard_map(
        per_device,
        mesh=fine,
        in_specs=(P(INTEG, TASK), P(TASK + INTEG, None), P(), P(INTEG + TASK, None)),
        out_specs=P(INTEG + TASK, None),
        check_vma=False,
    )
```

time: 1240 us -> 144 us (0.12)
  the two profiles are of different devices: /device:TPU:1 before, /device:TPU:32 now
where the time goes in v1:
time: 144 us; the launch traced here: 143 us
  blocking collectives  130 us (90%)
  Pallas kernels  6.54 us (5%)
  waiting for transfers between devices  2.25 us (2%)
  starting transfers between devices  1.91 us (1%)
  local copies, waits for them, and re-layouts  1.77 us (1%)
    all_to_all x1, blocking collectives, per_device(): parts = lax.all_to_all(messages, TASK, 0, 0, tiled=True).astype(jnp.float32)  77.6 us
    all_gather x3, blocking collectives, per_device(): packed = lax.all_gather(packed, axis, axis=0, tiled=True)  52.3 us
  transfers between devices with their start and end apart: 1, of which 1 were waited for; matrix products, arithmetic and copies ran while one was open for 0% of the time, Pallas kernels for 0%

profile of v1, /device:TPU:32, one launch (start us, length us, event | category | flops | bytes accessed | tf_op | source)
XLA Modules:
  0.0 143.3 jit_solution(14927982392453227083)
XLA Ops:
  0.0 1.7 %copy.6.mask_hbm = s32[768,8]{1,0:T(8,128)} copy(s32[768,8]{0,1:T(8,128)} %param.6) | data formatting | bytes 49152 | tf_op args[2]
  1.7 2.5 %compress.1 = bf16[96,256]{1,0:T(8,128)(2,1)} custom-call(s32[768,8]{1,0:T(8,128)} %copy.6.mask_hbm, bf16[96,1024]{1,0:T(8,128)(2,1)} %rows_ref.1), custom_call_target="tpu_custom_call" | custom-call | tf_op jit(solution)/shard_map/compress/pallas_call | solution.py:96
  4.2 0.0 copy-start.1
  4.2 17.0 %all_gather.9 = bf16[192,256]{1,0:T(8,128)(2,1)S(1)} all-gather(bf16[96,256]{1,0:T(8,128)(2,1)} %compress.1), channel_id=1, replica_groups=mesh['zh'=2,'y'=4,'x'=4,'z8'=2,'z4'=2,'z2'=2,'z1'=2,'c'=2] {'z8'}, dimensions={0}, use_global_device_ids=true | all-gather | bytes 147456 | tf_op jit(solution)/shard_map/all_gather | solution.py:105
  21.2 17.0 %all_gather.10 = bf16[384,256]{1,0:T(8,128)(2,1)S(1)} all-gather(bf16[192,256]{1,0:T(8,128)(2,1)S(1)} %all_gather.9), channel_id=1, replica_groups=mesh['zh'=2,'y'=4,'x'=4,'z8'=2,'z4'=2,'z2'=2,'z1'=2,'c'=2] {'z4'}, dimensions={0}, use_global_device_ids=true | all-gather | bytes 294912 | tf_op jit(solution)/shard_map/all_gather | solution.py:105
  38.1 0.0 copy-start
  38.1 18.3 %all_gather.11.own_ref = bf16[1536,256]{1,0:T(8,128)(2,1)S(1)} all-gather(bf16[384,256]{1,0:T(8,128)(2,1)S(1)} %all_gather.10), channel_id=1, replica_groups=mesh['zh'=2,'y'=4,'x'=4,'z8'=2,'z4'=2,'z2'=2,'z1'=2,'c'=2] {'z2','z1'}, dimensions={0}, use_global_device_ids=true | all-gather | bytes 983040 | tf_op jit(solution)/shard_map/all_gather | solution.py:105
  56.5 1.9 %collective-permute-start = (bf16[1536,256]{1,0:T(8,128)(2,1)S(1)}, bf16[1536,256]{1,0:T(8,128)(2,1)S(1)}, u32[]{:S(2)}, u32[]{:S(2)}) collective-permute-start(bf16[1536,256]{1,0:T(8,128)(2,1)S(1)} %all_gather.11.own_ref), channel_id=1, source_target_pairs={{0,1},{1,0},{2,3},{3,2},{4,5},{5,4},{6,7},{7,6},{8,9},{9,8},{10,11... | collective-permute-start | bytes 2359304 | tf_op jit(solution)/shard_map/ppermute | solution.py:106
  58.4 2.3 %collective-permute-done.other_ref = bf16[1536,256]{1,0:T(8,128)(2,1)S(1)} collective-permute-done((bf16[1536,256]{1,0:T(8,128)(2,1)S(1)}, bf16[1536,256]{1,0:T(8,128)(2,1)S(1)}, u32[]{:S(2)}, u32[]{:S(2)}) %collective-permute-start) | collective-permute-done | bytes 786464 | tf_op jit(solution)/shard_map/ppermute | solution.py:106
  60.6 0.0 copy-done.1
  60.7 0.0 copy-done
  60.7 2.2 %ladder.1 = f32[128,1152]{1,0:T(8,128)S(1)} custom-call(s32[768,8]{1,0:T(8,128)S(1)} %copy-done, bf16[128,3072]{1,0:T(8,128)(2,1)S(1)} %copy-done.1, bf16[1536,256]{1,0:T(8,128)(2,1)S(1)} %all_gather.11.own_ref, bf16[1536,256]{1,0:T(8,128)(2,1)S(1)} %collective-permute-done.other_ref), custom_call_target="tpu_custom_call" | custom-call | tf_op jit(solution)/shard_map/ladder/pallas_call | solution.py:107
  62.9 0.1 reshape.3
  63.0 77.6 %all_to_all.5 = f16[32,4,1152]{2,1,0:T(4,128)(2,1)S(1)} all-to-all(f16[32,4,1152]{2,1,0:T(4,128)(2,1)S(1)} %reshape.3), channel_id=1, replica_groups=mesh['zh'=2,'y'=4,'x'=4,'z8'=2,'z4'=2,'z2'=2,'z1'=2,'c'=2] {'zh','y','x'}, dimensions={0} | all-to-all | bytes 589824 | tf_op jit(solution)/shard_map/all_to_all | solution.py:122
  140.6 0.9 convert_element_type.7.parts_ref
  141.5 1.8 %combine.1 = f32[4,1024]{1,0:T(4,128)} custom-call(f32[32,4,1152]{2,1,0:T(4,128)} %convert_element_type.7.parts_ref, f32[4,1024]{1,0:T(4,128)} %residual_ref.1), custom_call_target="tpu_custom_call" | custom-call | tf_op jit(solution)/shard_map/combine/pallas_call | solution.py:123
  (1 shorter events, 0.0 us)
Async XLA Ops:
  4.2 56.5 %copy-start.1 = (bf16[128,3072]{1,0:T(8,128)(2,1)S(1)}, bf16[128,3072]{1,0:T(8,128)(2,1)}, u32[]{:S(2)}) copy-start(bf16[128,3072]{1,0:T(8,128)(2,1)} %amp_ref.1) | copy-start | bytes 2359300
  38.1 22.5 %copy-start = (s32[768,8]{1,0:T(8,128)S(1)}, s32[768,8]{1,0:T(8,128)}, u32[]{:S(2)}) copy-start(s32[768,8]{1,0:T(8,128)} %copy.6.mask_hbm) | copy-start | bytes 73732
  56.5 4.2 %collective-permute-start = (bf16[1536,256]{1,0:T(8,128)(2,1)S(1)}, bf16[1536,256]{1,0:T(8,128)(2,1)S(1)}, u32[]{:S(2)}, u32[]{:S(2)}) collective-permute-start(bf16[1536,256]{1,0:T(8,128)(2,1)S(1)} %all_gather.11.own_ref), channel_id=1, source_target_pairs={{0,1},{1,0},{2,3},{3,2},{4,5},{5,4},{6,7},{7,6},{8,9},{9,8},{10,11... | collective-permute-start | bytes 2359304 | tf_op jit(solution)/shard_map/ppermute | solution.py:106

commit v2 on v0

v2 whole, which is shorter than its diff:
```python
import functools

import jax
import jax.numpy as jnp
from jax import lax
from jax.experimental import pallas as pl
from jax.experimental.pallas import tpu as pltpu
from jax.sharding import Mesh
from jax.sharding import PartitionSpec as P

TILE = 128
ROWS = 96
GROUP = 32
TASK = ("zh", "y", "x")
PLANE = ("y", "x")
INTEG = ("z8", "z4", "z2", "z1", "c")
SIZES = (2, 4, 4, 2, 2, 2, 2, 2)
SWAP = ((0, 1), (1, 0))


def chip_of(slot):
    z2, z1, z4 = (slot >> 2) & 1, (slot >> 1) & 1, slot & 1
    return z4 * 4 + z2 * 2 + z1


def blocks_of(mask, tile):
    first, second, count = jnp.int32(0), jnp.int32(0), jnp.int32(0)
    for b in range(mask.shape[0]):
        one = mask[b, tile] != 0
        first = jnp.where(one & (count == 0), b, first)
        second = jnp.where(one & (count == 1), b, second)
        count = count + one.astype(jnp.int32)
    return first, second, count


def block_cols(block):
    return pl.ds(pl.multiple_of(block * TILE, TILE), TILE)


def compress_kernel(tiles, mask, rows_ref, out_ref):
    task, integ = lax.axis_index(TASK), lax.axis_index(INTEG)
    for g in range(ROWS // GROUP):
        tile = task * tiles + (integ * ROWS + g * GROUP) // TILE
        first, second, count = blocks_of(mask, tile)
        rows = pl.ds(g * GROUP, GROUP)
        for half, block in ((0, first), (1, second)):
            part = rows_ref[rows, block_cols(block)]
            out_ref[rows, pl.ds(half * TILE, TILE)] = jnp.where(count > half, part, jnp.zeros_like(part))


def ladder_kernel(tiles, flip, mask, amp_ref, near_ref, near_swapped_ref, far_ref, after_ref, out_ref, packed, total):
    core, z8, zh = lax.axis_index("c"), lax.axis_index("z8"), lax.axis_index("zh")
    for slot in range(8):
        rows = pl.ds(slot * ROWS, ROWS)
        near, far = z8 * 8 + chip_of(slot), (1 - z8) * 8 + chip_of(slot)
        for chip, which, ref in ((near, core, near_ref), (near, 1 - core, near_swapped_ref)):
            packed[pl.ds(pl.multiple_of((2 * chip + which) * ROWS, GROUP), ROWS), :] = ref[rows, :]
        for which in range(2):
            at = pl.multiple_of((2 * far + which) * ROWS, GROUP)
            packed[pl.ds(at, ROWS), :] = far_ref[pl.ds((which * 8 + slot) * ROWS, ROWS), :]
    pairs, width = total.shape
    half = 1 - zh if flip else zh
    amp_rows = pl.ds(pl.multiple_of(half * pairs, pairs), pairs)
    total[...] = jnp.zeros_like(total)
    for tile in range(tiles):
        first, second, _ = blocks_of(mask, lax.axis_index(TASK) * tiles + tile)
        cols = pl.ds(tile * TILE, TILE)
        part = jnp.dot(amp_ref[amp_rows, cols], packed[cols, :], preferred_element_type=jnp.float32)
        total[:, block_cols(first)] += part[:, :TILE]
        total[:, block_cols(second)] += part[:, TILE:]
    largest = jnp.max(jnp.abs(total[...]))
    exponent = jnp.floor(jnp.log2(jnp.maximum(jnp.full((8, TILE), largest), 2.0**-100))) - 10.0
    out_ref[:, :width] = total[...] * (0.5 * jnp.exp2(-exponent[:1, :1]))
    out_ref[:, width:] = jnp.broadcast_to(exponent[:1], (pairs, TILE))


def combine_kernel(parts_ref, start_ref, out_ref):
    width = out_ref.shape[1]
    total = start_ref[...]
    for i in range(parts_ref.shape[0]):
        total = total + parts_ref[i, :, :width] * jnp.exp2(parts_ref[i, :, width:])[:, :1]
    out_ref[...] = total


def per_device(amplitudes, integrals, block_mask, residual_in):
    cd_tiles, ab_tiles = block_mask.shape
    pairs, width = amplitudes.shape[0] // 2, ab_tiles * TILE
    tiles = cd_tiles // lax.axis_size(TASK)
    places = lax.axis_size(PLANE)
    smem_spec = pl.BlockSpec(memory_space=pltpu.SMEM)
    vmem_spec = pl.BlockSpec(memory_space=pltpu.VMEM)
    mask = block_mask.T
    gather = functools.partial(lax.all_gather, axis=0, tiled=True)

    own = pl.pallas_call(
        functools.partial(compress_kernel, tiles),
        out_shape=jax.ShapeDtypeStruct((ROWS, 2 * TILE), jnp.bfloat16),
        in_specs=[smem_spec, vmem_spec],
        out_specs=vmem_spec,
        name="compress",
    )(mask, integrals)
    across = lax.ppermute(own, "z8", SWAP)
    near = gather(gather(own, "z4"), ("z2", "z1"))
    near_swapped = lax.ppermute(near, "c", SWAP)
    far = gather(gather(gather(across, "z4"), ("z2", "z1")), "c")

    def reduced(flip, start, after):
        ladder = pl.pallas_call(
            functools.partial(ladder_kernel, tiles, flip),
            out_shape=jax.ShapeDtypeStruct((pairs, width + TILE), jnp.float32),
            in_specs=[smem_spec] + [vmem_spec] * 4 + [pl.BlockSpec(memory_space=pl.ANY)],
            out_specs=vmem_spec,
            scratch_shapes=[
                pltpu.VMEM((32 * ROWS, 2 * TILE), jnp.bfloat16),
                pltpu.VMEM((pairs, width), jnp.float32),
            ],
            compiler_params=pltpu.CompilerParams(vmem_limit_bytes=32 * 1024 * 1024),
            name="ladder",
        )(mask, amplitudes, near, near_swapped, far, after)
        messages = ladder.astype(jnp.float16).reshape(places, pairs // places, width + TILE)
        parts = lax.all_to_all(messages, PLANE, 0, 0, tiled=True).astype(jnp.float32)
        return pl.pallas_call(
            combine_kernel,
            out_shape=jax.ShapeDtypeStruct(residual_in.shape, jnp.float32),
            in_specs=[vmem_spec] * 2,
            out_specs=vmem_spec,
            name="combine",
        )(parts, start)

    theirs = reduced(True, jnp.zeros_like(residual_in), mask)
    received = lax.ppermute(theirs, "zh", SWAP)
    return reduced(False, residual_in, theirs) + received


def solution(mesh):
    fine = Mesh(mesh.devices.reshape(SIZES), TASK + INTEG)
    return jax.shard_map(
        per_device,
        mesh=fine,
        in_specs=(P(INTEG, TASK), P(TASK + INTEG, None), P(), P(INTEG + TASK, None)),
        out_specs=P(INTEG + TASK, None),
        check_vma=False,
    )
```

time: 1240 us -> 128 us (0.10); the launches traced: 1220 us -> 127 us
  waiting for transfers between devices: 1200 us -> 0.01 us
  blocking collectives: 0 us -> 66.6 us
  starting transfers between devices: 0.04 us -> 45.9 us
  between operations: 14.1 us -> 0.11 us
    unnamed x3 -> x0, waiting for transfers between devices: 852 us -> none
    all_gather x1 -> x0, waiting for transfers between devices: 344 us -> none  [per_device(): lax.all_gather(masked, 'integ', axis=0, tiled=True)]
    all_gather x0 -> x5, blocking collectives: none -> 53.1 us  [the longest x3 28.2 us: per_device(): far = gather(gather(gather(across, 'z4'), ('z2', 'z1')), 'c')]
    ppermute x0 -> x3, starting transfers between devices: none -> 42.3 us  [the longest x1 21.6 us: per_device(): received = lax.ppermute(theirs, 'zh', SWAP)]
    all_to_all x0 -> x1, blocking collectives: none -> 13.5 us  [reduced(): lax.all_to_all(messages, PLANE, 0, 0, tiled=True).astype(jnp.float32)]
  transfers between devices with their start and end apart: 2 -> 4, of which waited for: 2 -> 0; matrix products, arithmetic and copies ran while one was open for 0% -> 1% of each run, Pallas kernels for 0% -> 1%
where the time goes in v2:
time: 128 us; the launch traced here: 127 us
  blocking collectives  66.6 us (52%)
  starting transfers between devices  45.9 us (36%)
  Pallas kernels  9.21 us (7%)
  other arithmetic  2.91 us (2%)
  local copies, waits for them, and re-layouts  2.09 us (2%)
    all_gather x3, blocking collectives, per_device(): far = gather(gather(gather(across, 'z4'), ('z2', 'z1')), 'c')  28.2 us
    all_gather x2, blocking collectives, per_device(): near = gather(gather(own, 'z4'), ('z2', 'z1'))  25 us
    ppermute x1, starting transfers between devices, per_device(): received = lax.ppermute(theirs, 'zh', SWAP)  21.6 us
    ppermute x1, starting transfers between devices, per_device(): across = lax.ppermute(own, 'z8', SWAP)  16.3 us
    all_to_all x1, blocking collectives, reduced(): lax.all_to_all(messages, PLANE, 0, 0, tiled=True).astype(jnp.float32)  13.5 us
    ppermute x1, starting transfers between devices, per_device(): near_swapped = lax.ppermute(near, 'c', SWAP)  4.43 us
    pallas_call x2, Pallas kernels, reduced(): pl.pallas_call(functools.partial(ladder_kernel, tiles, flip), out_shape=j...  4.07 us
    all_to_all x1, starting transfers between devices, reduced(): lax.all_to_all(messages, PLANE, 0, 0, tiled=True).astype(jnp.float32)  3.65 us
  transfers between devices with their start and end apart: 4, of which 0 were waited for; matrix products, arithmetic and copies ran while one was open for 1% of the time, Pallas kernels for 1%

profile of v2, /device:TPU:1, one launch (start us, length us, event | category | flops | bytes accessed | tf_op | source)
XLA Modules:
  0.0 126.9 jit_solution(4351267869579581485)
XLA Ops:
  0.0 1.8 %compress.1 = bf16[96,256]{1,0:T(8,128)(2,1)} custom-call(s32[8,768]{1,0:T(8,128)} %bitcast.1, bf16[96,1024]{1,0:T(8,128)(2,1)} %rows_ref.1), custom_call_target="tpu_custom_call" | custom-call | tf_op jit(solution)/shard_map/compress/pallas_call | solution.py:95
  1.8 16.3 %collective-permute-start.1 = (bf16[96,256]{1,0:T(8,128)(2,1)}, bf16[96,256]{1,0:T(8,128)(2,1)S(1)}, u32[]{:S(2)}, u32[]{:S(2)}) collective-permute-start(bf16[96,256]{1,0:T(8,128)(2,1)} %compress.1), channel_id=1, source_target_pairs={{0,16},{16,0},{1,17},{17,1},{2,18},{18,2},{3,19},{19,3},{4,20},{20... | collective-permute-start | bytes 147464 | tf_op jit(solution)/shard_map/ppermute | solution.py:102
  18.1 9.3 %all_gather.15 = bf16[192,256]{1,0:T(8,128)(2,1)S(1)} all-gather(bf16[96,256]{1,0:T(8,128)(2,1)} %compress.1), channel_id=1, replica_groups=mesh['zh'=2,'y'=4,'x'=4,'z8'=2,'z4'=2,'z2'=2,'z1'=2,'c'=2] {'z4'}, dimensions={0}, use_global_device_ids=true | all-gather | bytes 147456 | tf_op jit(solution)/shard_map/all_gather | solution.py:103
  27.4 15.6 %all_gather.16.near_ref = bf16[768,256]{1,0:T(8,128)(2,1)S(1)} all-gather(bf16[192,256]{1,0:T(8,128)(2,1)S(1)} %all_gather.15), channel_id=1, replica_groups=mesh['zh'=2,'y'=4,'x'=4,'z8'=2,'z4'=2,'z2'=2,'z1'=2,'c'=2] {'z2','z1'}, dimensions={0}, use_global_device_ids=true | all-gather | bytes 491520 | tf_op jit(solution)/shard_map/all_gather | solution.py:103
  43.0 4.4 %collective-permute-start = (bf16[768,256]{1,0:T(8,128)(2,1)S(1)}, bf16[768,256]{1,0:T(8,128)(2,1)S(1)}, u32[]{:S(2)}, u32[]{:S(2)}) collective-permute-start(bf16[768,256]{1,0:T(8,128)(2,1)S(1)} %all_gather.16.near_ref), channel_id=1, source_target_pairs={{0,1},{1,0},{2,3},{3,2},{4,5},{5,4},{6,7},{7,6},{8,9},{9,8},{10,11... | collective-permute-start | bytes 1179656 | tf_op jit(solution)/shard_map/ppermute | solution.py:104
  47.5 0.0 collective-permute-done.1
  47.5 11.0 %all_gather.17 = bf16[192,256]{1,0:T(8,128)(2,1)S(1)} all-gather(bf16[96,256]{1,0:T(8,128)(2,1)S(1)} %collective-permute-done.1), channel_id=1, replica_groups=mesh['zh'=2,'y'=4,'x'=4,'z8'=2,'z4'=2,'z2'=2,'z1'=2,'c'=2] {'z4'}, dimensions={0}, use_global_device_ids=true | all-gather | bytes 147456 | tf_op jit(solution)/shard_map/all_gather | solution.py:105
  58.5 0.0 copy-start
  58.5 12.4 %all_gather.18 = bf16[768,256]{1,0:T(8,128)(2,1)S(1)} all-gather(bf16[192,256]{1,0:T(8,128)(2,1)S(1)} %all_gather.17), channel_id=1, replica_groups=mesh['zh'=2,'y'=4,'x'=4,'z8'=2,'z4'=2,'z2'=2,'z1'=2,'c'=2] {'z2','z1'}, dimensions={0}, use_global_device_ids=true | all-gather | bytes 491520 | tf_op jit(solution)/shard_map/all_gather | solution.py:105
  71.0 0.0 copy-start.1
  71.0 4.7 %all_gather.19.far_ref = bf16[1536,256]{1,0:T(8,128)(2,1)S(1)} all-gather(bf16[768,256]{1,0:T(8,128)(2,1)S(1)} %all_gather.18), channel_id=1, replica_groups=mesh['zh'=2,'y'=4,'x'=4,'z8'=2,'z4'=2,'z2'=2,'z1'=2,'c'=2] {'c'}, dimensions={0}, use_global_device_ids=true | all-gather | bytes 1179648 | tf_op jit(solution)/shard_map/all_gather | solution.py:105
  75.7 0.0 collective-permute-done.near_swapped_ref
  75.7 0.0 copy-done
  75.7 0.0 copy-done.1
  75.7 2.0 %ladder.2 = f32[64,1152]{1,0:T(8,128)S(1)} custom-call(s32[8,768]{1,0:T(8,128)S(1)} %bitcast.2, bf16[128,3072]{1,0:T(8,128)(2,1)S(1)} %copy-done, bf16[768,256]{1,0:T(8,128)(2,1)S(1)} %all_gather.16.near_ref, bf16[768,256]{1,0:T(8,128)(2,1)S(1)} %collective-permute-done.near_swapped_ref, bf16[1536,256]{1,0:T(8,128)(2,1)S(1)} %all_gather.19.far_ref, ...), custom_call_target="tpu_custom_call" | custom-call | tf_op jit(solution)/shard_map/ladder/pallas_call | solution.py:108
  77.7 0.1 reshape.6
  77.8 13.5 %all_to_all.10 = f16[16,4,1152]{2,1,0:T(4,128)(2,1)S(1)} all-to-all(f16[16,4,1152]{2,1,0:T(4,128)(2,1)S(1)} %reshape.6), channel_id=1, replica_groups=mesh['zh'=2,'y'=4,'x'=4,'z8'=2,'z4'=2,'z2'=2,'z1'=2,'c'=2] {'y','x'}, dimensions={0} | all-to-all | bytes 294912 | tf_op jit(solution)/shard_map/all_to_all | solution.py:121
  91.3 0.8 convert_element_type.13.parts_ref
  92.1 0.6 broadcast_in_dim.3.start_ref
  92.7 1.7 %combine.2.after_ref = f32[4,1024]{1,0:T(4,128)} custom-call(f32[16,4,1152]{2,1,0:T(4,128)} %convert_element_type.13.parts_ref, f32[4,1024]{1,0:T(4,128)} %broadcast_in_dim.3.start_ref), custom_call_target="tpu_custom_call" | custom-call | tf_op jit(solution)/shard_map/combine/pallas_call | solution.py:122
  94.3 0.0 copy-start.2
  94.3 0.7 copy-done.2
  95.0 2.0 %ladder.3 = f32[64,1152]{1,0:T(8,128)S(1)} custom-call(s32[8,768]{1,0:T(8,128)S(1)} %bitcast.4, bf16[128,3072]{1,0:T(8,128)(2,1)S(1)} %copy-done, bf16[768,256]{1,0:T(8,128)(2,1)S(1)} %all_gather.16.near_ref, bf16[768,256]{1,0:T(8,128)(2,1)S(1)} %collective-permute-done.near_swapped_ref, bf16[1536,256]{1,0:T(8,128)(2,1)S(1)} %all_gather.19.far_ref, ...), custom_call_target="tpu_custom_call" | custom-call | tf_op jit(solution)/shard_map/ladder/pallas_call | solution.py:108
  97.1 0.7 reshape.7
  97.8 0.0 copy-start.3
  97.8 3.6 %all-to-all-start.1 = ((f16[16,4,1152]{2,1,0:T(4,128)(2,1)}), f16[16,4,1152]{2,1,0:T(4,128)(2,1)S(1)}, u32[]{:S(2)}, u32[]{:S(2)}) async-start(f16[16,4,1152]{2,1,0:T(4,128)(2,1)} %reshape.7), calls=%async_computation.1 | async-start | bytes 294912 | tf_op jit(solution)/shard_map/all_to_all | solution.py:121
  101.5 0.0 copy-done.3
  101.5 21.6 %collective-permute-start.2 = (f32[4,1024]{1,0:T(4,128)S(1)}, f32[4,1024]{1,0:T(4,128)S(1)}, u32[]{:S(2)}, u32[]{:S(2)}) collective-permute-start(f32[4,1024]{1,0:T(4,128)S(1)} %copy-done.3), channel_id=1, source_target_pairs={{0,512},{512,0},{1,513},{513,1},{2,514},{514,2},{3,515},{515,3},{4... | collective-permute-start | bytes 49160 | tf_op jit(solution)/shard_map/ppermute | solution.py:131
  123.1 0.0 all-to-all-done.1
  123.1 0.8 convert_element_type.15.parts_ref
  123.9 1.7 %combine.3 = f32[4,1024]{1,0:T(4,128)} custom-call(f32[16,4,1152]{2,1,0:T(4,128)} %convert_element_type.15.parts_ref, f32[4,1024]{1,0:T(4,128)} %start_ref.1), custom_call_target="tpu_custom_call" | custom-call | tf_op jit(solution)/shard_map/combine/pallas_call | solution.py:122
  125.5 0.0 collective-permute-done.2
  125.5 1.3 %add.3 = f32[4,1024]{1,0:T(4,128)} add(f32[4,1024]{1,0:T(4,128)} %combine.3, f32[4,1024]{1,0:T(4,128)S(1)} %collective-permute-done.2) | non-fusion elementwise | flops 4096 | bytes 49152 | tf_op jit(solution)/shard_map/add | solution.py:132
  (2 shorter events, 0.0 us)
Async XLA Ops:
  1.8 45.7 %collective-permute-start.1 = (bf16[96,256]{1,0:T(8,128)(2,1)}, bf16[96,256]{1,0:T(8,128)(2,1)S(1)}, u32[]{:S(2)}, u32[]{:S(2)}) collective-permute-start(bf16[96,256]{1,0:T(8,128)(2,1)} %compress.1), channel_id=1, source_target_pairs={{0,16},{16,0},{1,17},{17,1},{2,18},{18,2},{3,19},{19,3},{4,20},{20... | collective-permute-start | bytes 147464 | tf_op jit(solution)/shard_map/ppermute | solution.py:102
  43.0 32.6 %collective-permute-start = (bf16[768,256]{1,0:T(8,128)(2,1)S(1)}, bf16[768,256]{1,0:T(8,128)(2,1)S(1)}, u32[]{:S(2)}, u32[]{:S(2)}) collective-permute-start(bf16[768,256]{1,0:T(8,128)(2,1)S(1)} %all_gather.16.near_ref), channel_id=1, source_target_pairs={{0,1},{1,0},{2,3},{3,2},{4,5},{5,4},{6,7},{7,6},{8,9},{9,8},{10,11... | collective-permute-start | bytes 1179656 | tf_op jit(solution)/shard_map/ppermute | solution.py:104
  58.5 17.2 %copy-start = (bf16[128,3072]{1,0:T(8,128)(2,1)S(1)}, bf16[128,3072]{1,0:T(8,128)(2,1)}, u32[]{:S(2)}) copy-start(bf16[128,3072]{1,0:T(8,128)(2,1)} %amp_ref.3) | copy-start | bytes 2359300
  71.0 4.7 %copy-start.1 = (s32[768,8]{0,1:T(8,128)S(1)}, s32[768,8]{0,1:T(8,128)}, u32[]{:S(2)}) copy-start(s32[768,8]{0,1:T(8,128)} %param.6) | copy-start | bytes 73732
  94.3 0.7 copy-start.2
  97.8 3.7 %copy-start.3 = (f32[4,1024]{1,0:T(4,128)S(1)}, f32[4,1024]{1,0:T(4,128)}, u32[]{:S(2)}) copy-start(f32[4,1024]{1,0:T(4,128)} %combine.2.after_ref) | copy-start | bytes 49156
  97.8 25.3 %all-to-all-start.1 = ((f16[16,4,1152]{2,1,0:T(4,128)(2,1)}), f16[16,4,1152]{2,1,0:T(4,128)(2,1)S(1)}, u32[]{:S(2)}, u32[]{:S(2)}) async-start(f16[16,4,1152]{2,1,0:T(4,128)(2,1)} %reshape.7), calls=%async_computation.1 | async-start | bytes 294912 | tf_op jit(solution)/shard_map/all_to_all | solution.py:121
  101.5 24.0 %collective-permute-start.2 = (f32[4,1024]{1,0:T(4,128)S(1)}, f32[4,1024]{1,0:T(4,128)S(1)}, u32[]{:S(2)}, u32[]{:S(2)}) collective-permute-start(f32[4,1024]{1,0:T(4,128)S(1)} %copy-done.3), channel_id=1, source_target_pairs={{0,512},{512,0},{1,513},{513,1},{2,514},{514,2},{3,515},{515,3},{4... | collective-permute-start | bytes 49160 | tf_op jit(solution)/shard_map/ppermute | solution.py:131

commit v3 on v2

v3 whole, which is shorter than its diff:
```python
import functools

import jax
import jax.numpy as jnp
from jax import lax
from jax.experimental import pallas as pl
from jax.experimental.pallas import tpu as pltpu
from jax.sharding import Mesh
from jax.sharding import PartitionSpec as P

TILE = 128
ROWS = 96
GROUP = 32
TASK = ("zh", "y", "x")
PLANE = ("y", "x")
INTEG = ("z8", "z4", "z2", "z1", "c")
SIZES = (2, 4, 4, 2, 2, 2, 2, 2)
SWAP = ((0, 1), (1, 0))


def chip_of(slot, z8):
    z2, z1, across, z4 = (slot >> 3) & 1, (slot >> 2) & 1, (slot >> 1) & 1, slot & 1
    return (1 - z8 if across else z8) * 8 + z4 * 4 + z2 * 2 + z1


def blocks_of(mask, tile):
    first, second, count = jnp.int32(0), jnp.int32(0), jnp.int32(0)
    for b in range(mask.shape[0]):
        one = mask[b, tile] != 0
        first = jnp.where(one & (count == 0), b, first)
        second = jnp.where(one & (count == 1), b, second)
        count = count + one.astype(jnp.int32)
    return first, second, count


def block_cols(block):
    return pl.ds(pl.multiple_of(block * TILE, TILE), TILE)


def compress_kernel(tiles, mask, rows_ref, out_ref):
    task, integ = lax.axis_index(TASK), lax.axis_index(INTEG)
    for g in range(ROWS // GROUP):
        tile = task * tiles + (integ * ROWS + g * GROUP) // TILE
        first, second, count = blocks_of(mask, tile)
        rows = pl.ds(g * GROUP, GROUP)
        for half, block in ((0, first), (1, second)):
            part = rows_ref[rows, block_cols(block)]
            out_ref[rows, pl.ds(half * TILE, TILE)] = jnp.where(count > half, part, jnp.zeros_like(part))


def ladder_kernel(tiles, mask, amp_ref, own_ref, other_ref, out_ref, packed, total):
    core, z8 = lax.axis_index("c"), lax.axis_index("z8")
    for slot in range(16):
        rows = pl.ds(slot * ROWS, ROWS)
        for which, ref in ((core, own_ref), (1 - core, other_ref)):
            at = pl.multiple_of((2 * chip_of(slot, z8) + which) * ROWS, GROUP)
            packed[pl.ds(at, ROWS), :] = ref[rows, :]
    pairs, width = total.shape
    total[...] = jnp.zeros_like(total)
    for tile in range(tiles):
        first, second, _ = blocks_of(mask, lax.axis_index(TASK) * tiles + tile)
        cols = pl.ds(tile * TILE, TILE)
        part = jnp.dot(amp_ref[:, cols], packed[cols, :], preferred_element_type=jnp.float32)
        total[:, block_cols(first)] += part[:, :TILE]
        total[:, block_cols(second)] += part[:, TILE:]
    largest = jnp.max(jnp.abs(total[...]))
    exponent = jnp.floor(jnp.log2(jnp.maximum(jnp.full((8, TILE), largest), 2.0**-100))) - 10.0
    scale = 0.5 * jnp.exp2(-exponent[:1, :1])
    places, rows = out_ref.shape[0], out_ref.shape[1] // 2
    for place in range(places):
        for zh in range(2):
            piece = total[pl.ds((zh * places + place) * rows, rows), :]
            out_ref[place, pl.ds(zh * rows, rows), :width] = piece * scale
        out_ref[place, :, width:] = exponent


def combine_kernel(parts_ref, residual_ref, mine_ref, theirs_ref):
    rows, width = residual_ref.shape
    total = jnp.zeros((2 * rows, width), jnp.float32)
    for i in range(parts_ref.shape[0]):
        total = total + parts_ref[i, :, :width] * jnp.exp2(parts_ref[i, :, width:])[:, :1]
    first = lax.axis_index("zh") == 0
    mine_ref[...] = residual_ref[...] + jnp.where(first, total[:rows], total[rows:])
    theirs_ref[...] = jnp.where(first, total[rows:], total[:rows])


def per_device(amplitudes, integrals, block_mask, residual_in):
    cd_tiles, ab_tiles = block_mask.shape
    pairs, width = amplitudes.shape[0], ab_tiles * TILE
    tiles = cd_tiles // lax.axis_size(TASK)
    places = lax.axis_size(PLANE)
    smem_spec = pl.BlockSpec(memory_space=pltpu.SMEM)
    vmem_spec = pl.BlockSpec(memory_space=pltpu.VMEM)
    mask = block_mask.T
    gather = functools.partial(lax.all_gather, axis=0, tiled=True)

    messages = (places, 2 * residual_in.shape[0], width + TILE)
    packed = pl.pallas_call(
        functools.partial(compress_kernel, tiles),
        out_shape=jax.ShapeDtypeStruct((ROWS, 2 * TILE), jnp.bfloat16),
        in_specs=[smem_spec, vmem_spec],
        out_specs=vmem_spec,
        name="compress",
    )(mask, integrals)
    across = lax.ppermute(packed, "z8", SWAP)
    own = gather(jnp.concatenate([gather(packed, "z4"), gather(across, "z4")]), ("z2", "z1"))
    other = lax.ppermute(own, "c", SWAP)
    ladder = pl.pallas_call(
        functools.partial(ladder_kernel, tiles),
        out_shape=jax.ShapeDtypeStruct(messages, jnp.float32),
        in_specs=[smem_spec] + [vmem_spec] * 3,
        out_specs=vmem_spec,
        scratch_shapes=[
            pltpu.VMEM((32 * ROWS, 2 * TILE), jnp.bfloat16),
            pltpu.VMEM((pairs, width), jnp.float32),
        ],
        compiler_params=pltpu.CompilerParams(vmem_limit_bytes=32 * 1024 * 1024),
        name="ladder",
    )(mask, amplitudes, own, other)
    parts = lax.all_to_all(ladder.astype(jnp.float16), PLANE, 0, 0, tiled=True)
    mine, theirs = pl.pallas_call(
        combine_kernel,
        out_shape=(jax.ShapeDtypeStruct(residual_in.shape, jnp.float32),) * 2,
        in_specs=[vmem_spec] * 2,
        out_specs=(vmem_spec, vmem_spec),
        name="combine",
    )(parts.astype(jnp.float32), residual_in)
    return mine + lax.ppermute(theirs, "zh", SWAP)


def solution(mesh):
    fine = Mesh(mesh.devices.reshape(SIZES), TASK + INTEG)
    return jax.shard_map(
        per_device,
        mesh=fine,
        in_specs=(P(INTEG, TASK), P(TASK + INTEG, None), P(), P(INTEG + TASK, None)),
        out_specs=P(INTEG + TASK, None),
        check_vma=False,
    )
```

time: 128 us -> 109 us (0.85)
  blocking collectives: 66.6 us -> 52.4 us
  waiting for transfers between devices: 0.01 us -> 4.44 us
  Pallas kernels: 9.21 us -> 6.17 us
  starting transfers between devices: 45.9 us -> 42.9 us
  local copies, waits for them, and re-layouts: 2.09 us -> 0.01 us
    all_gather x5 -> x3, blocking collectives: 53.1 us -> 37.4 us  [the longest x1 20.2 us: per_device(): gather(jnp.concatenate([gather(packed, 'z4'), gather(across, 'z4')]), ('z...]
    ppermute x3, waiting for transfers between devices: 0.01 us -> 4.44 us  [the longest x1 2.54 us: per_device(): return mine + lax.ppermute(theirs, 'zh', SWAP)]
    all_to_all x1 -> x0, starting transfers between devices: 3.65 us -> none  [reduced(): lax.all_to_all(messages, PLANE, 0, 0, tiled=True).astype(jnp.float32)]
    pallas_call x4 -> x2, Pallas kernels: 7.39 us -> 4.35 us  [the longest x1 2.56 us: per_device(): pl.pallas_call(functools.partial(ladder_kernel, tiles), out_shape=jax.Sha...]
    all_to_all x1, blocking collectives: 13.5 us -> 15 us  [per_device(): parts = lax.all_to_all(ladder.astype(jnp.float16), PLANE, 0, 0, tiled=True)]
  transfers between devices with their start and end apart: 4 -> 3, of which waited for: 0 -> 2; matrix products, arithmetic and copies ran while one was open for 1% -> 0% of each run, Pallas kernels for 1% -> 0%
where the time goes in v3:
time: 109 us; the launch traced here: 108 us
  blocking collectives  52.4 us (48%)
  starting transfers between devices  42.9 us (39%)
  Pallas kernels  6.17 us (6%)
  waiting for transfers between devices  4.44 us (4%)
  other arithmetic  2.24 us (2%)
    ppermute x1, starting transfers between devices, per_device(): return mine + lax.ppermute(theirs, 'zh', SWAP)  20.5 us
    all_gather x1, blocking collectives, per_device(): gather(jnp.concatenate([gather(packed, 'z4'), gather(across, 'z4')]), ('z...  20.2 us
    ppermute x1, starting transfers between devices, per_device(): across = lax.ppermute(packed, 'z8', SWAP)  16.3 us
    all_to_all x1, blocking collectives, per_device(): parts = lax.all_to_all(ladder.astype(jnp.float16), PLANE, 0, 0, tiled=True)  15 us
    all_gather x1, blocking collectives, per_device(): gather(packed, 'z4')  9.32 us
    all_gather x1, blocking collectives, per_device(): gather(across, 'z4')  7.87 us
    ppermute x1, starting transfers between devices, per_device(): other = lax.ppermute(own, 'c', SWAP)  6.21 us
    pallas_call x1, Pallas kernels, per_device(): pl.pallas_call(functools.partial(ladder_kernel, tiles), out_shape=jax.Sha...  2.56 us
  transfers between devices with their start and end apart: 3, of which 2 were waited for; matrix products, arithmetic and copies ran while one was open for 0% of the time, Pallas kernels for 0%

profile of v3, /device:TPU:1, one launch (start us, length us, event | category | flops | bytes accessed | tf_op | source)
XLA Modules:
  0.0 108.2 jit_solution(14906301157698691133)
XLA Ops:
  0.0 1.8 %compress.1 = bf16[96,256]{1,0:T(8,128)(2,1)} custom-call(s32[8,768]{1,0:T(8,128)} %bitcast.1, bf16[96,1024]{1,0:T(8,128)(2,1)} %rows_ref.1), custom_call_target="tpu_custom_call" | custom-call | tf_op jit(solution)/shard_map/compress/pallas_call | solution.py:98
  1.8 16.3 %collective-permute-start = (bf16[96,256]{1,0:T(8,128)(2,1)}, bf16[96,256]{1,0:T(8,128)(2,1)S(1)}, u32[]{:S(2)}, u32[]{:S(2)}) collective-permute-start(bf16[96,256]{1,0:T(8,128)(2,1)} %compress.1), channel_id=1, source_target_pairs={{0,16},{16,0},{1,17},{17,1},{2,18},{18,2},{3,19},{19,3},{4,20},{20... | collective-permute-start | bytes 147464 | tf_op jit(solution)/shard_map/ppermute | solution.py:105
  18.1 9.3 %all_gather.9 = bf16[192,256]{1,0:T(8,128)(2,1)S(1)} all-gather(bf16[96,256]{1,0:T(8,128)(2,1)} %compress.1), channel_id=1, replica_groups=mesh['zh'=2,'y'=4,'x'=4,'z8'=2,'z4'=2,'z2'=2,'z1'=2,'c'=2] {'z4'}, dimensions={0}, use_global_device_ids=true | all-gather | bytes 147456 | tf_op jit(solution)/shard_map/all_gather | solution.py:106
  27.4 0.0 copy-start
  27.4 0.0 collective-permute-done
  27.4 7.9 %all_gather.10 = bf16[192,256]{1,0:T(8,128)(2,1)S(1)} all-gather(bf16[96,256]{1,0:T(8,128)(2,1)S(1)} %collective-permute-done), channel_id=1, replica_groups=mesh['zh'=2,'y'=4,'x'=4,'z8'=2,'z4'=2,'z2'=2,'z1'=2,'c'=2] {'z4'}, dimensions={0}, use_global_device_ids=true | all-gather | bytes 147456 | tf_op jit(solution)/shard_map/all_gather | solution.py:106
  35.3 0.0 copy-start.1
  35.3 20.2 %all_gather.11.own_ref = bf16[1536,256]{1,0:T(8,128)(2,1)S(1)} all-gather(bf16[384,256]{1,0:T(8,128)(2,1)S(1)} %pad_maximum_fusion), channel_id=1, replica_groups=mesh['zh'=2,'y'=4,'x'=4,'z8'=2,'z4'=2,'z2'=2,'z1'=2,'c'=2] {'z2','z1'}, dimensions={0}, use_global_device_ids=true | all-gather | bytes 983040 | tf_op jit(solution)/shard_map/all_gather | solution.py:106
  55.5 6.2 %collective-permute-start.1 = (bf16[1536,256]{1,0:T(8,128)(2,1)S(1)}, bf16[1536,256]{1,0:T(8,128)(2,1)S(1)}, u32[]{:S(2)}, u32[]{:S(2)}) collective-permute-start(bf16[1536,256]{1,0:T(8,128)(2,1)S(1)} %all_gather.11.own_ref), channel_id=1, source_target_pairs={{0,1},{1,0},{2,3},{3,2},{4,5},{5,4},{6,7},{7,6},{8,9},{9,8},{10,11... | collective-permute-start | bytes 2359304 | tf_op jit(solution)/shard_map/ppermute | solution.py:107
  61.7 1.9 %collective-permute-done.1.other_ref = bf16[1536,256]{1,0:T(8,128)(2,1)S(1)} collective-permute-done((bf16[1536,256]{1,0:T(8,128)(2,1)S(1)}, bf16[1536,256]{1,0:T(8,128)(2,1)S(1)}, u32[]{:S(2)}, u32[]{:S(2)}) %collective-permute-start.1) | collective-permute-done | bytes 786464 | tf_op jit(solution)/shard_map/ppermute | solution.py:107
  63.6 0.0 copy-done
  63.6 0.0 copy-done.1
  63.6 2.6 %ladder.1 = f32[16,8,1152]{2,1,0:T(8,128)S(1)} custom-call(s32[8,768]{1,0:T(8,128)S(1)} %bitcast.2, bf16[128,3072]{1,0:T(8,128)(2,1)S(1)} %copy-done, bf16[1536,256]{1,0:T(8,128)(2,1)S(1)} %all_gather.11.own_ref, bf16[1536,256]{1,0:T(8,128)(2,1)S(1)} %collective-permute-done.1.other_ref), custom_call_target="tpu_custom_call" | custom-call | tf_op jit(solution)/shard_map/ladder/pallas_call | solution.py:108
  66.2 15.0 %all_to_all.5 = f16[16,8,1152]{2,1,0:T(8,128)(2,1)S(1)} all-to-all(f16[16,8,1152]{2,1,0:T(8,128)(2,1)S(1)} %convert_element_type.6), channel_id=1, replica_groups=mesh['zh'=2,'y'=4,'x'=4,'z8'=2,'z4'=2,'z2'=2,'z1'=2,'c'=2] {'y','x'}, dimensions={0} | all-to-all | bytes 589824 | tf_op jit(solution)/shard_map/all_to_all | solution.py:120
  81.2 0.9 convert_element_type.7.parts_ref
  82.1 1.8 %combine.1 = (f32[4,1024]{1,0:T(4,128)}, f32[4,1024]{1,0:T(4,128)}) custom-call(f32[16,8,1152]{2,1,0:T(8,128)} %convert_element_type.7.parts_ref, f32[4,1024]{1,0:T(4,128)} %residual_ref.1), custom_call_target="tpu_custom_call" | custom-call | tf_op jit(solution)/shard_map/combine/pallas_call | solution.py:121
  83.9 20.5 %collective-permute-start.2 = (f32[4,1024]{1,0:T(4,128)}, f32[4,1024]{1,0:T(4,128)S(1)}, u32[]{:S(2)}, u32[]{:S(2)}) collective-permute-start(f32[4,1024]{1,0:T(4,128)} %get-tuple-element.8), channel_id=1, source_target_pairs={{0,512},{512,0},{1,513},{513,1},{2,514},{514,2},{3,515},{515,3},{4... | collective-permute-start | bytes 49160 | tf_op jit(solution)/shard_map/ppermute | solution.py:128
  104.4 2.5 %collective-permute-done.2 = f32[4,1024]{1,0:T(4,128)S(1)} collective-permute-done((f32[4,1024]{1,0:T(4,128)}, f32[4,1024]{1,0:T(4,128)S(1)}, u32[]{:S(2)}, u32[]{:S(2)}) %collective-permute-start.2) | collective-permute-done | bytes 16416 | tf_op jit(solution)/shard_map/ppermute | solution.py:128
  106.9 1.3 %add.3 = f32[4,1024]{1,0:T(4,128)} add(f32[4,1024]{1,0:T(4,128)} %get-tuple-element.7, f32[4,1024]{1,0:T(4,128)S(1)} %collective-permute-done.2) | non-fusion elementwise | flops 4096 | bytes 49152 | tf_op jit(solution)/shard_map/add | solution.py:128
  (2 shorter events, 0.0 us)
Async XLA Ops:
  1.8 25.6 %collective-permute-start = (bf16[96,256]{1,0:T(8,128)(2,1)}, bf16[96,256]{1,0:T(8,128)(2,1)S(1)}, u32[]{:S(2)}, u32[]{:S(2)}) collective-permute-start(bf16[96,256]{1,0:T(8,128)(2,1)} %compress.1), channel_id=1, source_target_pairs={{0,16},{16,0},{1,17},{17,1},{2,18},{18,2},{3,19},{19,3},{4,20},{20... | collective-permute-start | bytes 147464 | tf_op jit(solution)/shard_map/ppermute | solution.py:105
  27.4 36.2 %copy-start = (bf16[128,3072]{1,0:T(8,128)(2,1)S(1)}, bf16[128,3072]{1,0:T(8,128)(2,1)}, u32[]{:S(2)}) copy-start(bf16[128,3072]{1,0:T(8,128)(2,1)} %amp_ref.1) | copy-start | bytes 2359300
  35.3 28.3 %copy-start.1 = (s32[768,8]{0,1:T(8,128)S(1)}, s32[768,8]{0,1:T(8,128)}, u32[]{:S(2)}) copy-start(s32[768,8]{0,1:T(8,128)} %param.6) | copy-start | bytes 73732
  55.5 8.1 %collective-permute-start.1 = (bf16[1536,256]{1,0:T(8,128)(2,1)S(1)}, bf16[1536,256]{1,0:T(8,128)(2,1)S(1)}, u32[]{:S(2)}, u32[]{:S(2)}) collective-permute-start(bf16[1536,256]{1,0:T(8,128)(2,1)S(1)} %all_gather.11.own_ref), channel_id=1, source_target_pairs={{0,1},{1,0},{2,3},{3,2},{4,5},{5,4},{6,7},{7,6},{8,9},{9,8},{10,11... | collective-permute-start | bytes 2359304 | tf_op jit(solution)/shard_map/ppermute | solution.py:107
  83.9 23.0 %collective-permute-start.2 = (f32[4,1024]{1,0:T(4,128)}, f32[4,1024]{1,0:T(4,128)S(1)}, u32[]{:S(2)}, u32[]{:S(2)}) collective-permute-start(f32[4,1024]{1,0:T(4,128)} %get-tuple-element.8), channel_id=1, source_target_pairs={{0,512},{512,0},{1,513},{513,1},{2,514},{514,2},{3,515},{515,3},{4... | collective-permute-start | bytes 49160 | tf_op jit(solution)/shard_map/ppermute | solution.py:128

commit v4 on v3

--- a/solution.py
+++ b/solution.py
@@ -16,11 +16,12 @@
 INTEG = ("z8", "z4", "z2", "z1", "c")
 SIZES = (2, 4, 4, 2, 2, 2, 2, 2)
 SWAP = ((0, 1), (1, 0))
+MIB = 1024 * 1024
 
 
-def chip_of(slot, z8):
-    z2, z1, across, z4 = (slot >> 3) & 1, (slot >> 2) & 1, (slot >> 1) & 1, slot & 1
-    return (1 - z8 if across else z8) * 8 + z4 * 4 + z2 * 2 + z1
+def chip_of(slot):
+    z2, z1, z4, z8 = (slot >> 3) & 1, (slot >> 2) & 1, (slot >> 1) & 1, slot & 1
+    return z8 * 8 + z4 * 4 + z2 * 2 + z1
 
 
 def blocks_of(mask, tile):
@@ -49,11 +50,11 @@
 
 
 def ladder_kernel(tiles, mask, amp_ref, own_ref, other_ref, out_ref, packed, total):
-    core, z8 = lax.axis_index("c"), lax.axis_index("z8")
+    core = lax.axis_index("c")
     for slot in range(16):
         rows = pl.ds(slot * ROWS, ROWS)
         for which, ref in ((core, own_ref), (1 - core, other_ref)):
-            at = pl.multiple_of((2 * chip_of(slot, z8) + which) * ROWS, GROUP)
+            at = pl.multiple_of((2 * chip_of(slot) + which) * ROWS, GROUP)
             packed[pl.ds(at, ROWS), :] = ref[rows, :]
     pairs, width = total.shape
     total[...] = jnp.zeros_like(total)
@@ -102,8 +103,7 @@
         out_specs=vmem_spec,
         name="compress",
     )(mask, integrals)
-    across = lax.ppermute(packed, "z8", SWAP)
-    own = gather(jnp.concatenate([gather(packed, "z4"), gather(across, "z4")]), ("z2", "z1"))
+    own = gather(gather(gather(packed, "z8"), "z4"), ("z2", "z1"))
     other = lax.ppermute(own, "c", SWAP)
     ladder = pl.pallas_call(
         functools.partial(ladder_kernel, tiles),
@@ -114,7 +114,7 @@
             pltpu.VMEM((32 * ROWS, 2 * TILE), jnp.bfloat16),
             pltpu.VMEM((pairs, width), jnp.float32),
         ],
-        compiler_params=pltpu.CompilerParams(vmem_limit_bytes=32 * 1024 * 1024),
+        compiler_params=pltpu.CompilerParams(vmem_limit_bytes=12 * MIB),
         name="ladder",
     )(mask, amplitudes, own, other)
     parts = lax.all_to_all(ladder.astype(jnp.float16), PLANE, 0, 0, tiled=True)
@@ -123,6 +123,7 @@
         out_shape=(jax.ShapeDtypeStruct(residual_in.shape, jnp.float32),) * 2,
         in_specs=[vmem_spec] * 2,
         out_specs=(vmem_spec, vmem_spec),
+        compiler_params=pltpu.CompilerParams(vmem_limit_bytes=4 * MIB),
         name="combine",
     )(parts.astype(jnp.float32), residual_in)
     return mine + lax.ppermute(theirs, "zh", SWAP)

time: 109 us -> 106 us (0.972)
  blocking collectives: 52.4 us -> 66.3 us
  starting transfers between devices: 42.9 us -> 29.9 us
  Pallas kernels: 6.17 us -> 4.56 us
  other arithmetic: 2.24 us -> 0.69 us
  waiting for transfers between devices: 4.44 us -> 3 us
    ppermute x1 -> x0, starting transfers between devices: 16.3 us -> none  [per_device(): across = lax.ppermute(packed, 'z8', SWAP)]
    all_gather x3, blocking collectives: 37.4 us -> 52 us  [per_device(): own = gather(gather(gather(packed, 'z8'), 'z4'), ('z2', 'z1'))]
    ppermute x1, starting transfers between devices: 20.5 us -> 23.6 us  [per_device(): return mine + lax.ppermute(theirs, 'zh', SWAP)]
    pallas_call x1, Pallas kernels: 1.79 us -> 0.11 us  [per_device(): pl.pallas_call(combine_kernel, out_shape=(jax.ShapeDtypeStruct(residual_i...]
    ppermute x1, waiting for transfers between devices: 2.54 us -> 1.11 us  [per_device(): return mine + lax.ppermute(theirs, 'zh', SWAP)]
  transfers between devices with their start and end apart: 3 -> 2, of which waited for: 2 -> 2; matrix products, arithmetic and copies ran while one was open for 0% -> 0% of each run, Pallas kernels for 0% -> 0%
where the time goes in v4:
time: 106 us; the launch traced here: 105 us
  blocking collectives  66.3 us (63%)
  starting transfers between devices  29.9 us (28%)
  Pallas kernels  4.56 us (4%)
  waiting for transfers between devices  3 us (3%)
    all_gather x3, blocking collectives, per_device(): own = gather(gather(gather(packed, 'z8'), 'z4'), ('z2', 'z1'))  52 us
    ppermute x1, starting transfers between devices, per_device(): return mine + lax.ppermute(theirs, 'zh', SWAP)  23.6 us
    all_to_all x1, blocking collectives, per_device(): parts = lax.all_to_all(ladder.astype(jnp.float16), PLANE, 0, 0, tiled=True)  14.3 us
    ppermute x1, starting transfers between devices, per_device(): other = lax.ppermute(own, 'c', SWAP)  6.26 us
    pallas_call x1, Pallas kernels, per_device(): pl.pallas_call(functools.partial(ladder_kernel, tiles), out_shape=jax.Sha...  2.5 us
  transfers between devices with their start and end apart: 2, of which 2 were waited for; matrix products, arithmetic and copies ran while one was open for 0% of the time, Pallas kernels for 0%

profile of v4, /device:TPU:1, one launch (start us, length us, event | category | flops | bytes accessed | tf_op | source)
XLA Modules:
  0.0 105.2 jit_solution(15276611523713414966)
XLA Ops:
  0.0 0.0 copy-start
  0.0 1.9 %compress.1 = bf16[96,256]{1,0:T(8,128)(2,1)} custom-call(s32[8,768]{1,0:T(8,128)} %bitcast.1, bf16[96,1024]{1,0:T(8,128)(2,1)} %rows_ref.1), custom_call_target="tpu_custom_call" | custom-call | tf_op jit(solution)/shard_map/compress/pallas_call | solution.py:99
  2.0 16.8 %all_gather.9 = bf16[192,256]{1,0:T(8,128)(2,1)S(1)} all-gather(bf16[96,256]{1,0:T(8,128)(2,1)} %compress.1), channel_id=1, replica_groups=mesh['zh'=2,'y'=4,'x'=4,'z8'=2,'z4'=2,'z2'=2,'z1'=2,'c'=2] {'z8'}, dimensions={0}, use_global_device_ids=true | all-gather | bytes 147456 | tf_op jit(solution)/shard_map/all_gather | solution.py:106
  18.7 12.3 %all_gather.10 = bf16[384,256]{1,0:T(8,128)(2,1)S(1)} all-gather(bf16[192,256]{1,0:T(8,128)(2,1)S(1)} %all_gather.9), channel_id=1, replica_groups=mesh['zh'=2,'y'=4,'x'=4,'z8'=2,'z4'=2,'z2'=2,'z1'=2,'c'=2] {'z4'}, dimensions={0}, use_global_device_ids=true | all-gather | bytes 294912 | tf_op jit(solution)/shard_map/all_gather | solution.py:106
  31.0 0.0 copy-start.1
  31.0 23.0 %all_gather.11.own_ref = bf16[1536,256]{1,0:T(8,128)(2,1)S(1)} all-gather(bf16[384,256]{1,0:T(8,128)(2,1)S(1)} %all_gather.10), channel_id=1, replica_groups=mesh['zh'=2,'y'=4,'x'=4,'z8'=2,'z4'=2,'z2'=2,'z1'=2,'c'=2] {'z2','z1'}, dimensions={0}, use_global_device_ids=true | all-gather | bytes 983040 | tf_op jit(solution)/shard_map/all_gather | solution.py:106
  54.0 6.3 %collective-permute-start = (bf16[1536,256]{1,0:T(8,128)(2,1)S(1)}, bf16[1536,256]{1,0:T(8,128)(2,1)S(1)}, u32[]{:S(2)}, u32[]{:S(2)}) collective-permute-start(bf16[1536,256]{1,0:T(8,128)(2,1)S(1)} %all_gather.11.own_ref), channel_id=1, source_target_pairs={{0,1},{1,0},{2,3},{3,2},{4,5},{5,4},{6,7},{7,6},{8,9},{9,8},{10,11... | collective-permute-start | bytes 2359304 | tf_op jit(solution)/shard_map/ppermute | solution.py:107
  60.2 1.9 %collective-permute-done.other_ref = bf16[1536,256]{1,0:T(8,128)(2,1)S(1)} collective-permute-done((bf16[1536,256]{1,0:T(8,128)(2,1)S(1)}, bf16[1536,256]{1,0:T(8,128)(2,1)S(1)}, u32[]{:S(2)}, u32[]{:S(2)}) %collective-permute-start) | collective-permute-done | bytes 786464 | tf_op jit(solution)/shard_map/ppermute | solution.py:107
  62.1 0.0 copy-done
  62.1 0.0 copy-done.1
  62.1 2.5 %ladder.1 = f32[16,8,1152]{2,1,0:T(8,128)S(1)} custom-call(s32[8,768]{1,0:T(8,128)S(1)} %bitcast.2, bf16[128,3072]{1,0:T(8,128)(2,1)S(1)} %copy-done, bf16[1536,256]{1,0:T(8,128)(2,1)S(1)} %all_gather.11.own_ref, bf16[1536,256]{1,0:T(8,128)(2,1)S(1)} %collective-permute-done.other_ref), custom_call_target="tpu_custom_call" | custom-call | tf_op jit(solution)/shard_map/ladder/pallas_call | solution.py:108
  64.7 14.3 %all_to_all.5 = f16[16,8,1152]{2,1,0:T(8,128)(2,1)S(1)} all-to-all(f16[16,8,1152]{2,1,0:T(8,128)(2,1)S(1)} %convert_element_type.6), channel_id=1, replica_groups=mesh['zh'=2,'y'=4,'x'=4,'z8'=2,'z4'=2,'z2'=2,'z1'=2,'c'=2] {'y','x'}, dimensions={0} | all-to-all | bytes 589824 | tf_op jit(solution)/shard_map/all_to_all | solution.py:120
  79.0 0.0 copy-start.2
  79.0 0.7 copy-done.2
  79.7 0.1 combine.1
  79.8 23.6 %collective-permute-start.1 = (f32[4,1024]{1,0:T(4,128)S(1)}, f32[4,1024]{1,0:T(4,128)S(1)}, u32[]{:S(2)}, u32[]{:S(2)}) collective-permute-start(f32[4,1024]{1,0:T(4,128)S(1)} %get-tuple-element.8), channel_id=1, source_target_pairs={{0,512},{512,0},{1,513},{513,1},{2,514},{514,2},{3,515},{515,3},{4... | collective-permute-start | bytes 49160 | tf_op jit(solution)/shard_map/ppermute | solution.py:129
  103.5 1.1 %collective-permute-done.1 = f32[4,1024]{1,0:T(4,128)S(1)} collective-permute-done((f32[4,1024]{1,0:T(4,128)S(1)}, f32[4,1024]{1,0:T(4,128)S(1)}, u32[]{:S(2)}, u32[]{:S(2)}) %collective-permute-start.1) | collective-permute-done | bytes 16416 | tf_op jit(solution)/shard_map/ppermute | solution.py:129
  104.6 0.6 add.3
  (2 shorter events, 0.1 us)
Async XLA Ops:
  0.0 62.1 %copy-start = (bf16[128,3072]{1,0:T(8,128)(2,1)S(1)}, bf16[128,3072]{1,0:T(8,128)(2,1)}, u32[]{:S(2)}) copy-start(bf16[128,3072]{1,0:T(8,128)(2,1)} %amp_ref.1) | copy-start | bytes 2359300
  31.0 31.1 %copy-start.1 = (s32[768,8]{0,1:T(8,128)S(1)}, s32[768,8]{0,1:T(8,128)}, u32[]{:S(2)}) copy-start(s32[768,8]{0,1:T(8,128)} %param.6) | copy-start | bytes 73732
  54.0 8.2 %collective-permute-start = (bf16[1536,256]{1,0:T(8,128)(2,1)S(1)}, bf16[1536,256]{1,0:T(8,128)(2,1)S(1)}, u32[]{:S(2)}, u32[]{:S(2)}) collective-permute-start(bf16[1536,256]{1,0:T(8,128)(2,1)S(1)} %all_gather.11.own_ref), channel_id=1, source_target_pairs={{0,1},{1,0},{2,3},{3,2},{4,5},{5,4},{6,7},{7,6},{8,9},{9,8},{10,11... | collective-permute-start | bytes 2359304 | tf_op jit(solution)/shard_map/ppermute | solution.py:107
  79.0 0.7 copy-start.2
  79.8 24.7 %collective-permute-start.1 = (f32[4,1024]{1,0:T(4,128)S(1)}, f32[4,1024]{1,0:T(4,128)S(1)}, u32[]{:S(2)}, u32[]{:S(2)}) collective-permute-start(f32[4,1024]{1,0:T(4,128)S(1)} %get-tuple-element.8), channel_id=1, source_target_pairs={{0,512},{512,0},{1,513},{513,1},{2,514},{514,2},{3,515},{515,3},{4... | collective-permute-start | bytes 49160 | tf_op jit(solution)/shard_map/ppermute | solution.py:129

commit v5 on v4

--- a/solution.py
+++ b/solution.py
@@ -75,13 +75,13 @@
         out_ref[place, :, width:] = exponent
 
 
-def combine_kernel(parts_ref, residual_ref, mine_ref, theirs_ref):
-    rows, width = residual_ref.shape
+def combine_kernel(parts_ref, mine_ref, theirs_ref):
+    rows, width = mine_ref.shape
     total = jnp.zeros((2 * rows, width), jnp.float32)
     for i in range(parts_ref.shape[0]):
         total = total + parts_ref[i, :, :width] * jnp.exp2(parts_ref[i, :, width:])[:, :1]
     first = lax.axis_index("zh") == 0
-    mine_ref[...] = residual_ref[...] + jnp.where(first, total[:rows], total[rows:])
+    mine_ref[...] = jnp.where(first, total[:rows], total[rows:])
     theirs_ref[...] = jnp.where(first, total[rows:], total[:rows])
 
 
@@ -121,12 +121,13 @@
     mine, theirs = pl.pallas_call(
         combine_kernel,
         out_shape=(jax.ShapeDtypeStruct(residual_in.shape, jnp.float32),) * 2,
-        in_specs=[vmem_spec] * 2,
+        in_specs=[vmem_spec],
         out_specs=(vmem_spec, vmem_spec),
         compiler_params=pltpu.CompilerParams(vmem_limit_bytes=4 * MIB),
         name="combine",
-    )(parts.astype(jnp.float32), residual_in)
-    return mine + lax.ppermute(theirs, "zh", SWAP)
+    )(parts.astype(jnp.float32))
+    both = lax.all_gather(theirs, "zh", axis=0)
+    return residual_in + (mine + jnp.where(lax.axis_index("zh") == 0, both[1], both[0]))
 
 
 def solution(mesh):

time: 106 us -> 105 us (level)
  starting transfers between devices: 29.9 us -> 12.3 us
  blocking collectives: 66.3 us -> 75.5 us
  waiting for transfers between devices: 3 us -> 10.3 us
    ppermute x1 -> x0, starting transfers between devices: 23.6 us -> none  [per_device(): return mine + lax.ppermute(theirs, 'zh', SWAP)]
    all_gather x0 -> x1, blocking collectives: none -> 23.5 us  [per_device(): both = lax.all_gather(theirs, 'zh', axis=0)]
    all_to_all x1 -> x0, blocking collectives: 14.3 us -> none  [per_device(): parts = lax.all_to_all(ladder.astype(jnp.float16), PLANE, 0, 0, tiled=True)]
    all_to_all x0 -> x1, waiting for transfers between devices: none -> 8.45 us  [per_device(): parts = lax.all_to_all(ladder.astype(jnp.float16), PLANE, 0, 0, tiled=True)]
    all_to_all x0 -> x1, starting transfers between devices: none -> 6.04 us  [per_device(): parts = lax.all_to_all(ladder.astype(jnp.float16), PLANE, 0, 0, tiled=True)]
    ppermute x1 -> x0, waiting for transfers between devices: 1.11 us -> none  [per_device(): return mine + lax.ppermute(theirs, 'zh', SWAP)]
where the time goes in v5:
time: 105 us; the launch traced here: 104 us
  blocking collectives  75.5 us (72%)
  starting transfers between devices  12.3 us (12%)
  waiting for transfers between devices  10.3 us (10%)
  Pallas kernels  4.56 us (4%)
  other arithmetic  1.39 us (1%)
    all_gather x3, blocking collectives, per_device(): own = gather(gather(gather(packed, 'z8'), 'z4'), ('z2', 'z1'))  52 us
    all_gather x1, blocking collectives, per_device(): both = lax.all_gather(theirs, 'zh', axis=0)  23.5 us
    all_to_all x1, waiting for transfers between devices, per_device(): parts = lax.all_to_all(ladder.astype(jnp.float16), PLANE, 0, 0, tiled=True)  8.45 us
    ppermute x1, starting transfers between devices, per_device(): other = lax.ppermute(own, 'c', SWAP)  6.26 us
    all_to_all x1, starting transfers between devices, per_device(): parts = lax.all_to_all(ladder.astype(jnp.float16), PLANE, 0, 0, tiled=True)  6.04 us
    pallas_call x1, Pallas kernels, per_device(): pl.pallas_call(functools.partial(ladder_kernel, tiles), out_shape=jax.Sha...  2.5 us
  transfers between devices with their start and end apart: 2, of which 2 were waited for; matrix products, arithmetic and copies ran while one was open for 0% of the time, Pallas kernels for 0%

profile of v5, /device:TPU:1, one launch (start us, length us, event | category | flops | bytes accessed | tf_op | source)
XLA Modules:
  0.0 104.2 jit_solution(11768026539471742972)
XLA Ops:
  0.0 0.0 copy-start
  0.0 1.9 %compress.1 = bf16[96,256]{1,0:T(8,128)(2,1)} custom-call(s32[8,768]{1,0:T(8,128)} %bitcast.8, bf16[96,1024]{1,0:T(8,128)(2,1)} %rows_ref.1), custom_call_target="tpu_custom_call" | custom-call | tf_op jit(solution)/shard_map/compress/pallas_call | solution.py:99
  1.9 16.8 %all_gather.15 = bf16[192,256]{1,0:T(8,128)(2,1)S(1)} all-gather(bf16[96,256]{1,0:T(8,128)(2,1)} %compress.1), channel_id=1, replica_groups=mesh['zh'=2,'y'=4,'x'=4,'z8'=2,'z4'=2,'z2'=2,'z1'=2,'c'=2] {'z8'}, dimensions={0}, use_global_device_ids=true | all-gather | bytes 147456 | tf_op jit(solution)/shard_map/all_gather | solution.py:106
  18.7 12.3 %all_gather.16 = bf16[384,256]{1,0:T(8,128)(2,1)S(1)} all-gather(bf16[192,256]{1,0:T(8,128)(2,1)S(1)} %all_gather.15), channel_id=1, replica_groups=mesh['zh'=2,'y'=4,'x'=4,'z8'=2,'z4'=2,'z2'=2,'z1'=2,'c'=2] {'z4'}, dimensions={0}, use_global_device_ids=true | all-gather | bytes 294912 | tf_op jit(solution)/shard_map/all_gather | solution.py:106
  31.0 0.0 copy-start.1
  31.0 23.0 %all_gather.17.own_ref = bf16[1536,256]{1,0:T(8,128)(2,1)S(1)} all-gather(bf16[384,256]{1,0:T(8,128)(2,1)S(1)} %all_gather.16), channel_id=1, replica_groups=mesh['zh'=2,'y'=4,'x'=4,'z8'=2,'z4'=2,'z2'=2,'z1'=2,'c'=2] {'z2','z1'}, dimensions={0}, use_global_device_ids=true | all-gather | bytes 983040 | tf_op jit(solution)/shard_map/all_gather | solution.py:106
  54.0 6.3 %collective-permute-start = (bf16[1536,256]{1,0:T(8,128)(2,1)S(1)}, bf16[1536,256]{1,0:T(8,128)(2,1)S(1)}, u32[]{:S(2)}, u32[]{:S(2)}) collective-permute-start(bf16[1536,256]{1,0:T(8,128)(2,1)S(1)} %all_gather.17.own_ref), channel_id=1, source_target_pairs={{0,1},{1,0},{2,3},{3,2},{4,5},{5,4},{6,7},{7,6},{8,9},{9,8},{10,11... | collective-permute-start | bytes 2359304 | tf_op jit(solution)/shard_map/ppermute | solution.py:107
  60.2 1.9 %collective-permute-done.other_ref = bf16[1536,256]{1,0:T(8,128)(2,1)S(1)} collective-permute-done((bf16[1536,256]{1,0:T(8,128)(2,1)S(1)}, bf16[1536,256]{1,0:T(8,128)(2,1)S(1)}, u32[]{:S(2)}, u32[]{:S(2)}) %collective-permute-start) | collective-permute-done | bytes 786464 | tf_op jit(solution)/shard_map/ppermute | solution.py:107
  62.1 0.0 copy-done
  62.1 0.0 copy-done.1
  62.1 2.5 %ladder.1 = f32[16,8,1152]{2,1,0:T(8,128)S(1)} custom-call(s32[8,768]{1,0:T(8,128)S(1)} %bitcast.9, bf16[128,3072]{1,0:T(8,128)(2,1)S(1)} %copy-done, bf16[1536,256]{1,0:T(8,128)(2,1)S(1)} %all_gather.17.own_ref, bf16[1536,256]{1,0:T(8,128)(2,1)S(1)} %collective-permute-done.other_ref), custom_call_target="tpu_custom_call" | custom-call | tf_op jit(solution)/shard_map/ladder/pallas_call | solution.py:108
  64.6 0.7 convert_element_type.6
  65.4 6.0 %all-to-all-start = ((f16[16,8,1152]{2,1,0:T(8,128)(2,1)}), f16[16,8,1152]{2,1,0:T(8,128)(2,1)S(1)}, u32[]{:S(2)}, u32[]{:S(2)}) async-start(f16[16,8,1152]{2,1,0:T(8,128)(2,1)} %convert_element_type.6), calls=%async_computation | async-start | bytes 589824 | tf_op jit(solution)/shard_map/all_to_all | solution.py:120
  71.4 8.5 %all-to-all-done = f16[16,8,1152]{2,1,0:T(8,128)(2,1)S(1)} async-done(((f16[16,8,1152]{2,1,0:T(8,128)(2,1)}), f16[16,8,1152]{2,1,0:T(8,128)(2,1)S(1)}, u32[]{:S(2)}, u32[]{:S(2)}) %all-to-all-start) | async-done | bytes 294944 | tf_op jit(solution)/shard_map/all_to_all | solution.py:120
  79.9 0.1 combine.1
  80.0 0.0 copy-start.2
  80.1 23.5 %all-gather.1 = f32[2,4,1024]{2,1,0:T(4,128)S(1)} all-gather(f32[1,4,1024]{2,1,0:T(4,128)S(1)} %bitcast.10), channel_id=2, replica_groups=mesh['zh'=2,'y'=4,'x'=4,'z8'=2,'z4'=2,'z2'=2,'z1'=2,'c'=2] {'zh'}, dimensions={0}, use_global_device_ids=true | all-gather | bytes 49152 | tf_op jit(solution)/shard_map/all_gather | solution.py:129
  103.5 0.0 copy-done.2
  103.5 0.6 fusion.2
  (1 shorter events, 0.0 us)
Async XLA Ops:
  0.0 62.1 %copy-start = (bf16[128,3072]{1,0:T(8,128)(2,1)S(1)}, bf16[128,3072]{1,0:T(8,128)(2,1)}, u32[]{:S(2)}) copy-start(bf16[128,3072]{1,0:T(8,128)(2,1)} %amp_ref.1) | copy-start | bytes 2359300
  31.0 31.1 %copy-start.1 = (s32[768,8]{0,1:T(8,128)S(1)}, s32[768,8]{0,1:T(8,128)}, u32[]{:S(2)}) copy-start(s32[768,8]{0,1:T(8,128)} %param.6) | copy-start | bytes 73732
  54.0 8.2 %collective-permute-start = (bf16[1536,256]{1,0:T(8,128)(2,1)S(1)}, bf16[1536,256]{1,0:T(8,128)(2,1)S(1)}, u32[]{:S(2)}, u32[]{:S(2)}) collective-permute-start(bf16[1536,256]{1,0:T(8,128)(2,1)S(1)} %all_gather.17.own_ref), channel_id=1, source_target_pairs={{0,1},{1,0},{2,3},{3,2},{4,5},{5,4},{6,7},{7,6},{8,9},{9,8},{10,11... | collective-permute-start | bytes 2359304 | tf_op jit(solution)/shard_map/ppermute | solution.py:107
  65.4 14.5 %all-to-all-start = ((f16[16,8,1152]{2,1,0:T(8,128)(2,1)}), f16[16,8,1152]{2,1,0:T(8,128)(2,1)S(1)}, u32[]{:S(2)}, u32[]{:S(2)}) async-start(f16[16,8,1152]{2,1,0:T(8,128)(2,1)} %convert_element_type.6), calls=%async_computation | async-start | bytes 589824 | tf_op jit(solution)/shard_map/all_to_all | solution.py:120
  80.0 23.5 %copy-start.2 = (f32[4,1024]{1,0:T(4,128)S(1)}, f32[4,1024]{1,0:T(4,128)}, u32[]{:S(2)}) copy-start(f32[4,1024]{1,0:T(4,128)} %param.7) | copy-start | bytes 49156

commit v6 on v5

--- a/solution.py
+++ b/solution.py
@@ -16,12 +16,13 @@
 INTEG = ("z8", "z4", "z2", "z1", "c")
 SIZES = (2, 4, 4, 2, 2, 2, 2, 2)
 SWAP = ((0, 1), (1, 0))
+RING = (0, 1, 3, 2)
+WINDOW = 2 * TILE
 MIB = 1024 * 1024
 
 
 def chip_of(slot):
-    z2, z1, z4, z8 = (slot >> 3) & 1, (slot >> 2) & 1, (slot >> 1) & 1, slot & 1
-    return z8 * 8 + z4 * 4 + z2 * 2 + z1
+    return (slot & 1) * 8 + ((slot >> 1) & 1) * 4 + RING[slot >> 2]
 
 
 def blocks_of(mask, tile):
@@ -34,32 +35,47 @@
     return first, second, count
 
 
+def mask_copy(mask_hbm, mask, sem, tiles):
+    tile = lax.axis_index(TASK) * tiles
+    base = jnp.minimum(tile // TILE, mask_hbm.shape[1] // TILE - WINDOW // TILE) * TILE
+    window = mask_hbm.at[:, pl.ds(pl.multiple_of(base, TILE), WINDOW)]
+    return pltpu.make_async_copy(window, mask, sem), tile - base
+
+
 def block_cols(block):
     return pl.ds(pl.multiple_of(block * TILE, TILE), TILE)
 
 
-def compress_kernel(tiles, mask, rows_ref, out_ref):
-    task, integ = lax.axis_index(TASK), lax.axis_index(INTEG)
-    for g in range(ROWS // GROUP):
-        tile = task * tiles + (integ * ROWS + g * GROUP) // TILE
-        first, second, count = blocks_of(mask, tile)
+def compress_kernel(tiles, mask_hbm, rows_hbm, out_ref, mask, rows_ref, mask_sem, rows_sem):
+    mask_in, origin = mask_copy(mask_hbm, mask, mask_sem, tiles)
+    rows_in = pltpu.make_async_copy(rows_hbm, rows_ref, rows_sem)
+    mask_in.start()
+    rows_in.start()
+    mask_in.wait()
+    integ = lax.axis_index(INTEG)
+    groups = [blocks_of(mask, origin + (integ * ROWS + g * GROUP) // TILE) for g in range(ROWS // GROUP)]
+    rows_in.wait()
+    for g, (first, second, count) in enumerate(groups):
         rows = pl.ds(g * GROUP, GROUP)
         for half, block in ((0, first), (1, second)):
             part = rows_ref[rows, block_cols(block)]
             out_ref[rows, pl.ds(half * TILE, TILE)] = jnp.where(count > half, part, jnp.zeros_like(part))
 
 
-def ladder_kernel(tiles, mask, amp_ref, own_ref, other_ref, out_ref, packed, total):
+def ladder_kernel(tiles, mask_hbm, amp_ref, own_ref, other_ref, out_ref, mask, packed, total, mask_sem):
+    mask_in, origin = mask_copy(mask_hbm, mask, mask_sem, tiles)
+    mask_in.start()
     core = lax.axis_index("c")
     for slot in range(16):
         rows = pl.ds(slot * ROWS, ROWS)
         for which, ref in ((core, own_ref), (1 - core, other_ref)):
             at = pl.multiple_of((2 * chip_of(slot) + which) * ROWS, GROUP)
             packed[pl.ds(at, ROWS), :] = ref[rows, :]
+    mask_in.wait()
     pairs, width = total.shape
     total[...] = jnp.zeros_like(total)
     for tile in range(tiles):
-        first, second, _ = blocks_of(mask, lax.axis_index(TASK) * tiles + tile)
+        first, second, _ = blocks_of(mask, origin + tile)
         cols = pl.ds(tile * TILE, TILE)
         part = jnp.dot(amp_ref[:, cols], packed[cols, :], preferred_element_type=jnp.float32)
         total[:, block_cols(first)] += part[:, :TILE]
@@ -75,12 +91,14 @@
         out_ref[place, :, width:] = exponent
 
 
-def combine_kernel(parts_ref, mine_ref, theirs_ref):
+def combine_kernel(parts_ref, mine_ref, theirs_ref, zh_ref):
     rows, width = mine_ref.shape
     total = jnp.zeros((2 * rows, width), jnp.float32)
     for i in range(parts_ref.shape[0]):
         total = total + parts_ref[i, :, :width] * jnp.exp2(parts_ref[i, :, width:])[:, :1]
-    first = lax.axis_index("zh") == 0
+    zh = lax.axis_index("zh")
+    first = zh == 0
+    zh_ref[...] = jnp.full(zh_ref.shape, zh, jnp.int32)
     mine_ref[...] = jnp.where(first, total[:rows], total[rows:])
     theirs_ref[...] = jnp.where(first, total[rows:], total[:rows])
 
@@ -90,7 +108,7 @@
     pairs, width = amplitudes.shape[0], ab_tiles * TILE
     tiles = cd_tiles // lax.axis_size(TASK)
     places = lax.axis_size(PLANE)
-    smem_spec = pl.BlockSpec(memory_space=pltpu.SMEM)
+    hbm_spec = pl.BlockSpec(memory_space=pltpu.HBM)
     vmem_spec = pl.BlockSpec(memory_space=pltpu.VMEM)
     mask = block_mask.T
     gather = functools.partial(lax.all_gather, axis=0, tiled=True)
@@ -99,35 +117,45 @@
     packed = pl.pallas_call(
         functools.partial(compress_kernel, tiles),
         out_shape=jax.ShapeDtypeStruct((ROWS, 2 * TILE), jnp.bfloat16),
-        in_specs=[smem_spec, vmem_spec],
+        in_specs=[hbm_spec, hbm_spec],
         out_specs=vmem_spec,
+        scratch_shapes=[
+            pltpu.SMEM((ab_tiles, WINDOW), jnp.int32),
+            pltpu.VMEM(integrals.shape, jnp.bfloat16),
+            pltpu.SemaphoreType.DMA,
+            pltpu.SemaphoreType.DMA,
+        ],
         name="compress",
     )(mask, integrals)
-    own = gather(gather(gather(packed, "z8"), "z4"), ("z2", "z1"))
+    cores, upper = lax.axis_size("c"), lax.axis_size(("z8", "z4"))
+    rings = [[(z * 4 + place) * cores + core for place in RING] for z in range(upper) for core in range(cores)]
+    own = gather(gather(gather(packed, "z8"), "z4"), INTEG, axis_index_groups=rings)
     other = lax.ppermute(own, "c", SWAP)
     ladder = pl.pallas_call(
         functools.partial(ladder_kernel, tiles),
         out_shape=jax.ShapeDtypeStruct(messages, jnp.float32),
-        in_specs=[smem_spec] + [vmem_spec] * 3,
+        in_specs=[hbm_spec] + [vmem_spec] * 3,
         out_specs=vmem_spec,
         scratch_shapes=[
+            pltpu.SMEM((ab_tiles, WINDOW), jnp.int32),
             pltpu.VMEM((32 * ROWS, 2 * TILE), jnp.bfloat16),
             pltpu.VMEM((pairs, width), jnp.float32),
+            pltpu.SemaphoreType.DMA,
         ],
         compiler_params=pltpu.CompilerParams(vmem_limit_bytes=12 * MIB),
         name="ladder",
     )(mask, amplitudes, own, other)
     parts = lax.all_to_all(ladder.astype(jnp.float16), PLANE, 0, 0, tiled=True)
-    mine, theirs = pl.pallas_call(
+    mine, theirs, zh = pl.pallas_call(
         combine_kernel,
-        out_shape=(jax.ShapeDtypeStruct(residual_in.shape, jnp.float32),) * 2,
+        out_shape=tuple(jax.ShapeDtypeStruct(residual_in.shape, t) for t in (jnp.float32, jnp.float32, jnp.int32)),
         in_specs=[vmem_spec],
-        out_specs=(vmem_spec, vmem_spec),
+        out_specs=(vmem_spec,) * 3,
         compiler_params=pltpu.CompilerParams(vmem_limit_bytes=4 * MIB),
         name="combine",
     )(parts.astype(jnp.float32))
     both = lax.all_gather(theirs, "zh", axis=0)
-    return residual_in + (mine + jnp.where(lax.axis_index("zh") == 0, both[1], both[0]))
+    return residual_in + (mine + jnp.where(zh == 0, both[1], both[0]))
 
 
 def solution(mesh):

time: 105 us -> 101 us (0.962)
  blocking collectives: 75.5 us -> 88.2 us
  waiting for transfers between devices: 10.3 us -> 1.89 us
  starting transfers between devices: 12.3 us -> 5.18 us
    all_to_all x0 -> x1, blocking collectives: none -> 13.9 us  [per_device(): parts = lax.all_to_all(ladder.astype(jnp.float16), PLANE, 0, 0, tiled=True)]
    all_to_all x1 -> x0, waiting for transfers between devices: 8.45 us -> none  [per_device(): parts = lax.all_to_all(ladder.astype(jnp.float16), PLANE, 0, 0, tiled=True)]
    all_to_all x1 -> x0, starting transfers between devices: 6.04 us -> none  [per_device(): parts = lax.all_to_all(ladder.astype(jnp.float16), PLANE, 0, 0, tiled=True)]
    ppermute x1, starting transfers between devices: 6.26 us -> 5.18 us  [per_device(): other = lax.ppermute(own, 'c', SWAP)]
    all_gather x1, blocking collectives: 23.5 us -> 22.4 us  [per_device(): both = lax.all_gather(theirs, 'zh', axis=0)]
  transfers between devices with their start and end apart: 2 -> 1, of which waited for: 2 -> 1; matrix products, arithmetic and copies ran while one was open for 0% -> 0% of each run, Pallas kernels for 0% -> 0%
where the time goes in v6:
time: 101 us; the launch traced here: 100 us
  blocking collectives  88.2 us (87%)
  starting transfers between devices  5.18 us (5%)
  Pallas kernels  4.04 us (4%)
  waiting for transfers between devices  1.89 us (2%)
    all_gather x1, blocking collectives, per_device(): gather(gather(gather(packed, 'z8'), 'z4'), INTEG, axis_index_groups=rings)  22.9 us
    all_gather x1, blocking collectives, per_device(): both = lax.all_gather(theirs, 'zh', axis=0)  22.4 us
    all_gather x1, blocking collectives, per_device(): gather(packed, 'z8')  16.8 us
    all_to_all x1, blocking collectives, per_device(): parts = lax.all_to_all(ladder.astype(jnp.float16), PLANE, 0, 0, tiled=True)  13.9 us
    all_gather x1, blocking collectives, per_device(): gather(gather(packed, 'z8'), 'z4')  12.3 us
    ppermute x1, starting transfers between devices, per_device(): other = lax.ppermute(own, 'c', SWAP)  5.18 us
    pallas_call x1, Pallas kernels, per_device(): pl.pallas_call(functools.partial(ladder_kernel, tiles), out_shape=jax.Sha...  2.25 us
  transfers between devices with their start and end apart: 1, of which 1 were waited for; matrix products, arithmetic and copies ran while one was open for 0% of the time, Pallas kernels for 0%

profile of v6, /device:TPU:1, one launch (start us, length us, event | category | flops | bytes accessed | tf_op | source)
XLA Modules:
  0.0 100.1 jit_solution(3959617163795758025)
XLA Ops:
  0.0 0.0 copy-start
  0.0 1.7 %compress.1 = bf16[96,256]{1,0:T(8,128)(2,1)} custom-call(s32[8,768]{1,0:T(8,128)} %bitcast.14, bf16[96,1024]{1,0:T(8,128)(2,1)} %rows_hbm.1), custom_call_target="tpu_custom_call" | custom-call | tf_op jit(solution)/shard_map/compress/pallas_call | solution.py:117
  1.7 16.8 %all_gather.15 = bf16[192,256]{1,0:T(8,128)(2,1)S(1)} all-gather(bf16[96,256]{1,0:T(8,128)(2,1)} %compress.1), channel_id=1, replica_groups=mesh['zh'=2,'y'=4,'x'=4,'z8'=2,'z4'=2,'z2'=2,'z1'=2,'c'=2] {'z8'}, dimensions={0}, use_global_device_ids=true | all-gather | bytes 147456 | tf_op jit(solution)/shard_map/all_gather | solution.py:132
  18.5 12.3 %all_gather.16 = bf16[384,256]{1,0:T(8,128)(2,1)S(1)} all-gather(bf16[192,256]{1,0:T(8,128)(2,1)S(1)} %all_gather.15), channel_id=1, replica_groups=mesh['zh'=2,'y'=4,'x'=4,'z8'=2,'z4'=2,'z2'=2,'z1'=2,'c'=2] {'z4'}, dimensions={0}, use_global_device_ids=true | all-gather | bytes 294912 | tf_op jit(solution)/shard_map/all_gather | solution.py:132
  30.8 0.0 copy-start.1
  30.8 22.9 %all_gather.17.own_ref = bf16[1536,256]{1,0:T(8,128)(2,1)S(1)} all-gather(bf16[384,256]{1,0:T(8,128)(2,1)S(1)} %all_gather.16), channel_id=1, replica_groups={{0,2,6,4},{1,3,7,5},{8,10,14,12},{9,11,15,13},{16,18,22,20},{17,19,23,2..., dimensions={0}, use_global_device_ids=true | all-gather | bytes 983040 | tf_op jit(solution)/shard_map/all_gather | solution.py:132
  53.6 5.2 %collective-permute-start = (bf16[1536,256]{1,0:T(8,128)(2,1)S(1)}, bf16[1536,256]{1,0:T(8,128)(2,1)S(1)}, u32[]{:S(2)}, u32[]{:S(2)}) collective-permute-start(bf16[1536,256]{1,0:T(8,128)(2,1)S(1)} %all_gather.17.own_ref), channel_id=1, source_target_pairs={{0,1},{1,0},{2,3},{3,2},{4,5},{5,4},{6,7},{7,6},{8,9},{9,8},{10,11... | collective-permute-start | bytes 2359304 | tf_op jit(solution)/shard_map/ppermute | solution.py:133
  58.8 1.9 %collective-permute-done.other_ref = bf16[1536,256]{1,0:T(8,128)(2,1)S(1)} collective-permute-done((bf16[1536,256]{1,0:T(8,128)(2,1)S(1)}, bf16[1536,256]{1,0:T(8,128)(2,1)S(1)}, u32[]{:S(2)}, u32[]{:S(2)}) %collective-permute-start) | collective-permute-done | bytes 786464 | tf_op jit(solution)/shard_map/ppermute | solution.py:133
  60.7 0.0 copy-done
  60.7 0.0 copy-done.1
  60.7 2.2 %ladder.1 = f32[16,8,1152]{2,1,0:T(8,128)S(1)} custom-call(s32[8,768]{1,0:T(8,128)S(1)} %bitcast.15, bf16[128,3072]{1,0:T(8,128)(2,1)S(1)} %copy-done, bf16[1536,256]{1,0:T(8,128)(2,1)S(1)} %all_gather.17.own_ref, bf16[1536,256]{1,0:T(8,128)(2,1)S(1)} %collective-permute-done.other_ref), custom_call_target="tpu_custom_call" | custom-call | tf_op jit(solution)/shard_map/ladder/pallas_call | solution.py:134
  63.0 13.9 %all_to_all.5 = f16[16,8,1152]{2,1,0:T(8,128)(2,1)S(1)} all-to-all(f16[16,8,1152]{2,1,0:T(8,128)(2,1)S(1)} %convert_element_type.6), channel_id=1, replica_groups=mesh['zh'=2,'y'=4,'x'=4,'z8'=2,'z4'=2,'z2'=2,'z1'=2,'c'=2] {'y','x'}, dimensions={0} | all-to-all | bytes 589824 | tf_op jit(solution)/shard_map/all_to_all | solution.py:148
  76.9 0.1 combine.1
  77.1 0.0 copy-start.2
  77.1 22.4 %all-gather.1 = f32[2,4,1024]{2,1,0:T(4,128)S(1)} all-gather(f32[1,4,1024]{2,1,0:T(4,128)S(1)} %bitcast.16), channel_id=2, replica_groups=mesh['zh'=2,'y'=4,'x'=4,'z8'=2,'z4'=2,'z2'=2,'z1'=2,'c'=2] {'zh'}, dimensions={0}, use_global_device_ids=true | all-gather | bytes 49152 | tf_op jit(solution)/shard_map/all_gather | solution.py:157
  99.5 0.0 copy-done.2
  99.5 0.6 fusion.2
  (2 shorter events, 0.1 us)
Async XLA Ops:
  0.0 60.7 %copy-start = (bf16[128,3072]{1,0:T(8,128)(2,1)S(1)}, bf16[128,3072]{1,0:T(8,128)(2,1)}, u32[]{:S(2)}) copy-start(bf16[128,3072]{1,0:T(8,128)(2,1)} %amp_ref.1) | copy-start | bytes 2359300
  30.8 30.0 %copy-start.1 = (s32[768,8]{0,1:T(8,128)S(1)}, s32[768,8]{0,1:T(8,128)}, u32[]{:S(2)}) copy-start(s32[768,8]{0,1:T(8,128)} %param.6) | copy-start | bytes 73732
  53.6 7.1 %collective-permute-start = (bf16[1536,256]{1,0:T(8,128)(2,1)S(1)}, bf16[1536,256]{1,0:T(8,128)(2,1)S(1)}, u32[]{:S(2)}, u32[]{:S(2)}) collective-permute-start(bf16[1536,256]{1,0:T(8,128)(2,1)S(1)} %all_gather.17.own_ref), channel_id=1, source_target_pairs={{0,1},{1,0},{2,3},{3,2},{4,5},{5,4},{6,7},{7,6},{8,9},{9,8},{10,11... | collective-permute-start | bytes 2359304 | tf_op jit(solution)/shard_map/ppermute | solution.py:133
  77.1 22.4 %copy-start.2 = (f32[4,1024]{1,0:T(4,128)S(1)}, f32[4,1024]{1,0:T(4,128)}, u32[]{:S(2)}) copy-start(f32[4,1024]{1,0:T(4,128)} %param.7) | copy-start | bytes 49156

commit v7 on v6

--- a/solution.py
+++ b/solution.py
@@ -13,16 +13,13 @@
 GROUP = 32
 TASK = ("zh", "y", "x")
 PLANE = ("y", "x")
-INTEG = ("z8", "z4", "z2", "z1", "c")
-SIZES = (2, 4, 4, 2, 2, 2, 2, 2)
+INTEG = ("z", "c")
+SIZES = (2, 4, 4, 16, 2)
 SWAP = ((0, 1), (1, 0))
-RING = (0, 1, 3, 2)
+CHIPS = 16
+RING = (0, *range(1, CHIPS, 2), *range(CHIPS - 2, 0, -2))
 WINDOW = 2 * TILE
 MIB = 1024 * 1024
-
-
-def chip_of(slot):
-    return (slot & 1) * 8 + ((slot >> 1) & 1) * 4 + RING[slot >> 2]
 
 
 def blocks_of(mask, tile):
@@ -66,10 +63,10 @@
     mask_in, origin = mask_copy(mask_hbm, mask, mask_sem, tiles)
     mask_in.start()
     core = lax.axis_index("c")
-    for slot in range(16):
+    for slot in range(CHIPS):
         rows = pl.ds(slot * ROWS, ROWS)
         for which, ref in ((core, own_ref), (1 - core, other_ref)):
-            at = pl.multiple_of((2 * chip_of(slot) + which) * ROWS, GROUP)
+            at = pl.multiple_of((2 * RING[slot] + which) * ROWS, GROUP)
             packed[pl.ds(at, ROWS), :] = ref[rows, :]
     mask_in.wait()
     pairs, width = total.shape
@@ -111,8 +108,6 @@
     hbm_spec = pl.BlockSpec(memory_space=pltpu.HBM)
     vmem_spec = pl.BlockSpec(memory_space=pltpu.VMEM)
     mask = block_mask.T
-    gather = functools.partial(lax.all_gather, axis=0, tiled=True)
-
     messages = (places, 2 * residual_in.shape[0], width + TILE)
     packed = pl.pallas_call(
         functools.partial(compress_kernel, tiles),
@@ -127,9 +122,9 @@
         ],
         name="compress",
     )(mask, integrals)
-    cores, upper = lax.axis_size("c"), lax.axis_size(("z8", "z4"))
-    rings = [[(z * 4 + place) * cores + core for place in RING] for z in range(upper) for core in range(cores)]
-    own = gather(gather(gather(packed, "z8"), "z4"), INTEG, axis_index_groups=rings)
+    cores = lax.axis_size("c")
+    rings = [[chip * cores + core for chip in RING] for core in range(cores)]
+    own = lax.all_gather(packed, INTEG, axis=0, tiled=True, axis_index_groups=rings)
     other = lax.ppermute(own, "c", SWAP)
     ladder = pl.pallas_call(
         functools.partial(ladder_kernel, tiles),

time: 101 us -> 98.2 us (0.972)
  blocking collectives: 88.2 us -> 84.8 us
    all_gather x3 -> x1, blocking collectives: 52 us -> 47.3 us  [per_device(): lax.all_gather(packed, INTEG, axis=0, tiled=True, axis_index_groups=rings)]
    all_to_all x1, blocking collectives: 13.9 us -> 15.9 us  [per_device(): parts = lax.all_to_all(ladder.astype(jnp.float16), PLANE, 0, 0, tiled=True)]
where the time goes in v7:
time: 98.2 us; the launch traced here: 97.1 us
  blocking collectives  84.8 us (86%)
  starting transfers between devices  5.55 us (6%)
  Pallas kernels  4.03 us (4%)
  waiting for transfers between devices  1.89 us (2%)
    all_gather x1, blocking collectives, per_device(): lax.all_gather(packed, INTEG, axis=0, tiled=True, axis_index_groups=rings)  47.3 us
    all_gather x1, blocking collectives, per_device(): both = lax.all_gather(theirs, 'zh', axis=0)  21.6 us
    all_to_all x1, blocking collectives, per_device(): parts = lax.all_to_all(ladder.astype(jnp.float16), PLANE, 0, 0, tiled=True)  15.9 us
    ppermute x1, starting transfers between devices, per_device(): other = lax.ppermute(own, 'c', SWAP)  5.55 us
    pallas_call x1, Pallas kernels, per_device(): pl.pallas_call(functools.partial(ladder_kernel, tiles), out_shape=jax.Sha...  2.25 us
  transfers between devices with their start and end apart: 1, of which 1 were waited for; matrix products, arithmetic and copies ran while one was open for 0% of the time, Pallas kernels for 0%

profile of v7, /device:TPU:1, one launch (start us, length us, event | category | flops | bytes accessed | tf_op | source)
XLA Modules:
  0.0 97.1 jit_solution(11749338599780839589)
XLA Ops:
  0.0 0.0 copy-start
  0.0 1.7 %compress.1 = bf16[96,256]{1,0:T(8,128)(2,1)} custom-call(s32[8,768]{1,0:T(8,128)} %bitcast.14, bf16[96,1024]{1,0:T(8,128)(2,1)} %rows_hbm.1), custom_call_target="tpu_custom_call" | custom-call | tf_op jit(solution)/shard_map/compress/pallas_call | solution.py:112
  1.7 0.0 copy-start.1
  1.7 47.3 %all_gather.9.own_ref = bf16[1536,256]{1,0:T(8,128)(2,1)S(1)} all-gather(bf16[96,256]{1,0:T(8,128)(2,1)} %compress.1), channel_id=1, replica_groups={{0,2,6,10,14,18,22,26,30,28,24,20,16,12,8,4},{1,3,7,11,15,19,23,27,31,2..., dimensions={0}, use_global_device_ids=true | all-gather | bytes 835584 | tf_op jit(solution)/shard_map/all_gather | solution.py:127
  49.0 5.6 %collective-permute-start = (bf16[1536,256]{1,0:T(8,128)(2,1)S(1)}, bf16[1536,256]{1,0:T(8,128)(2,1)S(1)}, u32[]{:S(2)}, u32[]{:S(2)}) collective-permute-start(bf16[1536,256]{1,0:T(8,128)(2,1)S(1)} %all_gather.9.own_ref), channel_id=1, source_target_pairs={{0,1},{1,0},{2,3},{3,2},{4,5},{5,4},{6,7},{7,6},{8,9},{9,8},{10,11... | collective-permute-start | bytes 2359304 | tf_op jit(solution)/shard_map/ppermute | solution.py:128
  54.6 1.9 %collective-permute-done.other_ref = bf16[1536,256]{1,0:T(8,128)(2,1)S(1)} collective-permute-done((bf16[1536,256]{1,0:T(8,128)(2,1)S(1)}, bf16[1536,256]{1,0:T(8,128)(2,1)S(1)}, u32[]{:S(2)}, u32[]{:S(2)}) %collective-permute-start) | collective-permute-done | bytes 786464 | tf_op jit(solution)/shard_map/ppermute | solution.py:128
  56.4 0.0 copy-done
  56.4 0.0 copy-done.1
  56.4 2.3 %ladder.1 = f32[16,8,1152]{2,1,0:T(8,128)S(1)} custom-call(s32[8,768]{1,0:T(8,128)S(1)} %bitcast.15, bf16[128,3072]{1,0:T(8,128)(2,1)S(1)} %copy-done, bf16[1536,256]{1,0:T(8,128)(2,1)S(1)} %all_gather.9.own_ref, bf16[1536,256]{1,0:T(8,128)(2,1)S(1)} %collective-permute-done.other_ref), custom_call_target="tpu_custom_call" | custom-call | tf_op jit(solution)/shard_map/ladder/pallas_call | solution.py:129
  58.8 15.9 %all_to_all.5 = f16[16,8,1152]{2,1,0:T(8,128)(2,1)S(1)} all-to-all(f16[16,8,1152]{2,1,0:T(8,128)(2,1)S(1)} %convert_element_type.6), channel_id=1, replica_groups=mesh['zh'=2,'y'=4,'x'=4,'z'=16,'c'=2] {'y','x'}, dimensions={0} | all-to-all | bytes 589824 | tf_op jit(solution)/shard_map/all_to_all | solution.py:143
  74.7 0.1 combine.1
  74.8 0.0 copy-start.2
  74.9 21.6 %all-gather.1 = f32[2,4,1024]{2,1,0:T(4,128)S(1)} all-gather(f32[1,4,1024]{2,1,0:T(4,128)S(1)} %bitcast.16), channel_id=2, replica_groups=mesh['zh'=2,'y'=4,'x'=4,'z'=16,'c'=2] {'zh'}, dimensions={0}, use_global_device_ids=true | all-gather | bytes 49152 | tf_op jit(solution)/shard_map/all_gather | solution.py:152
  96.5 0.0 copy-done.2
  96.5 0.6 fusion.2
  (2 shorter events, 0.1 us)
Async XLA Ops:
  0.0 56.4 %copy-start = (bf16[128,3072]{1,0:T(8,128)(2,1)S(1)}, bf16[128,3072]{1,0:T(8,128)(2,1)}, u32[]{:S(2)}) copy-start(bf16[128,3072]{1,0:T(8,128)(2,1)} %amp_ref.1) | copy-start | bytes 2359300
  1.7 54.8 %copy-start.1 = (s32[768,8]{0,1:T(8,128)S(1)}, s32[768,8]{0,1:T(8,128)}, u32[]{:S(2)}) copy-start(s32[768,8]{0,1:T(8,128)} %param.6) | copy-start | bytes 73732
  49.0 7.4 %collective-permute-start = (bf16[1536,256]{1,0:T(8,128)(2,1)S(1)}, bf16[1536,256]{1,0:T(8,128)(2,1)S(1)}, u32[]{:S(2)}, u32[]{:S(2)}) collective-permute-start(bf16[1536,256]{1,0:T(8,128)(2,1)S(1)} %all_gather.9.own_ref), channel_id=1, source_target_pairs={{0,1},{1,0},{2,3},{3,2},{4,5},{5,4},{6,7},{7,6},{8,9},{9,8},{10,11... | collective-permute-start | bytes 2359304 | tf_op jit(solution)/shard_map/ppermute | solution.py:128
  74.8 21.6 %copy-start.2 = (f32[4,1024]{1,0:T(4,128)S(1)}, f32[4,1024]{1,0:T(4,128)}, u32[]{:S(2)}) copy-start(f32[4,1024]{1,0:T(4,128)} %param.7) | copy-start | bytes 49156

commit v8 on v7

--- a/solution.py
+++ b/solution.py
@@ -18,6 +18,7 @@
 SWAP = ((0, 1), (1, 0))
 CHIPS = 16
 RING = (0, *range(1, CHIPS, 2), *range(CHIPS - 2, 0, -2))
+RINGS = (RING, RING[::-1])
 WINDOW = 2 * TILE
 MIB = 1024 * 1024
 
@@ -66,7 +67,8 @@
     for slot in range(CHIPS):
         rows = pl.ds(slot * ROWS, ROWS)
         for which, ref in ((core, own_ref), (1 - core, other_ref)):
-            at = pl.multiple_of((2 * RING[slot] + which) * ROWS, GROUP)
+            chip = jnp.where(which == 0, RINGS[0][slot], RINGS[1][slot])
+            at = pl.multiple_of((2 * chip + which) * ROWS, GROUP)
             packed[pl.ds(at, ROWS), :] = ref[rows, :]
     mask_in.wait()
     pairs, width = total.shape
@@ -123,7 +125,7 @@
         name="compress",
     )(mask, integrals)
     cores = lax.axis_size("c")
-    rings = [[chip * cores + core for chip in RING] for core in range(cores)]
+    rings = [[chip * cores + core for chip in ring] for core, ring in enumerate(RINGS)]
     own = lax.all_gather(packed, INTEG, axis=0, tiled=True, axis_index_groups=rings)
     other = lax.ppermute(own, "c", SWAP)
     ladder = pl.pallas_call(

time: 98.2 us -> 98.3 us (level)
  starting transfers between devices: 5.55 us -> 9.22 us
  blocking collectives: 84.8 us -> 81.9 us
    ppermute x1, starting transfers between devices: 5.55 us -> 9.22 us  [per_device(): other = lax.ppermute(own, 'c', SWAP)]
    all_gather x1, blocking collectives: 47.3 us -> 44.5 us  [per_device(): lax.all_gather(packed, INTEG, axis=0, tiled=True, axis_index_groups=rings)]
where the time goes in v8:
time: 98.3 us; the launch traced here: 97.8 us
  blocking collectives  81.9 us (83%)
  starting transfers between devices  9.22 us (9%)
  Pallas kernels  4.05 us (4%)
  waiting for transfers between devices  1.89 us (2%)
    all_gather x1, blocking collectives, per_device(): lax.all_gather(packed, INTEG, axis=0, tiled=True, axis_index_groups=rings)  44.5 us
    all_gather x1, blocking collectives, per_device(): both = lax.all_gather(theirs, 'zh', axis=0)  21.6 us
    all_to_all x1, blocking collectives, per_device(): parts = lax.all_to_all(ladder.astype(jnp.float16), PLANE, 0, 0, tiled=True)  15.8 us
    ppermute x1, starting transfers between devices, per_device(): other = lax.ppermute(own, 'c', SWAP)  9.22 us
    pallas_call x1, Pallas kernels, per_device(): pl.pallas_call(functools.partial(ladder_kernel, tiles), out_shape=jax.Sha...  2.27 us
  transfers between devices with their start and end apart: 1, of which 1 were waited for; matrix products, arithmetic and copies ran while one was open for 0% of the time, Pallas kernels for 0%

profile of v8, /device:TPU:1, one launch (start us, length us, event | category | flops | bytes accessed | tf_op | source)
XLA Modules:
  0.0 97.8 jit_solution(6054468995010792352)
XLA Ops:
  0.0 0.0 copy-start
  0.0 1.7 %compress.1 = bf16[96,256]{1,0:T(8,128)(2,1)} custom-call(s32[8,768]{1,0:T(8,128)} %bitcast.14, bf16[96,1024]{1,0:T(8,128)(2,1)} %rows_hbm.1), custom_call_target="tpu_custom_call" | custom-call | tf_op jit(solution)/shard_map/compress/pallas_call | solution.py:114
  1.7 0.0 copy-start.1
  1.7 44.5 %all_gather.9.own_ref = bf16[1536,256]{1,0:T(8,128)(2,1)S(1)} all-gather(bf16[96,256]{1,0:T(8,128)(2,1)} %compress.1), channel_id=1, replica_groups={{0,2,6,10,14,18,22,26,30,28,24,20,16,12,8,4},{5,9,13,17,21,25,29,31,27,..., dimensions={0}, use_global_device_ids=true | all-gather | bytes 835584 | tf_op jit(solution)/shard_map/all_gather | solution.py:129
  46.2 9.2 %collective-permute-start = (bf16[1536,256]{1,0:T(8,128)(2,1)S(1)}, bf16[1536,256]{1,0:T(8,128)(2,1)S(1)}, u32[]{:S(2)}, u32[]{:S(2)}) collective-permute-start(bf16[1536,256]{1,0:T(8,128)(2,1)S(1)} %all_gather.9.own_ref), channel_id=1, source_target_pairs={{0,1},{1,0},{2,3},{3,2},{4,5},{5,4},{6,7},{7,6},{8,9},{9,8},{10,11... | collective-permute-start | bytes 2359304 | tf_op jit(solution)/shard_map/ppermute | solution.py:130
  55.4 1.9 %collective-permute-done.other_ref = bf16[1536,256]{1,0:T(8,128)(2,1)S(1)} collective-permute-done((bf16[1536,256]{1,0:T(8,128)(2,1)S(1)}, bf16[1536,256]{1,0:T(8,128)(2,1)S(1)}, u32[]{:S(2)}, u32[]{:S(2)}) %collective-permute-start) | collective-permute-done | bytes 786464 | tf_op jit(solution)/shard_map/ppermute | solution.py:130
  57.3 0.0 copy-done
  57.3 0.0 copy-done.1
  57.3 2.3 %ladder.1 = f32[16,8,1152]{2,1,0:T(8,128)S(1)} custom-call(s32[8,768]{1,0:T(8,128)S(1)} %bitcast.15, bf16[128,3072]{1,0:T(8,128)(2,1)S(1)} %copy-done, bf16[1536,256]{1,0:T(8,128)(2,1)S(1)} %all_gather.9.own_ref, bf16[1536,256]{1,0:T(8,128)(2,1)S(1)} %collective-permute-done.other_ref), custom_call_target="tpu_custom_call" | custom-call | tf_op jit(solution)/shard_map/ladder/pallas_call | solution.py:131
  59.6 15.8 %all_to_all.5 = f16[16,8,1152]{2,1,0:T(8,128)(2,1)S(1)} all-to-all(f16[16,8,1152]{2,1,0:T(8,128)(2,1)S(1)} %convert_element_type.6), channel_id=1, replica_groups=mesh['zh'=2,'y'=4,'x'=4,'z'=16,'c'=2] {'y','x'}, dimensions={0} | all-to-all | bytes 589824 | tf_op jit(solution)/shard_map/all_to_all | solution.py:145
  75.4 0.1 combine.1
  75.6 0.0 copy-start.2
  75.6 21.6 %all-gather.1 = f32[2,4,1024]{2,1,0:T(4,128)S(1)} all-gather(f32[1,4,1024]{2,1,0:T(4,128)S(1)} %bitcast.16), channel_id=2, replica_groups=mesh['zh'=2,'y'=4,'x'=4,'z'=16,'c'=2] {'zh'}, dimensions={0}, use_global_device_ids=true | all-gather | bytes 49152 | tf_op jit(solution)/shard_map/all_gather | solution.py:154
  97.2 0.0 copy-done.2
  97.2 0.6 fusion.2
  (2 shorter events, 0.1 us)
Async XLA Ops:
  0.0 57.3 %copy-start = (bf16[128,3072]{1,0:T(8,128)(2,1)S(1)}, bf16[128,3072]{1,0:T(8,128)(2,1)}, u32[]{:S(2)}) copy-start(bf16[128,3072]{1,0:T(8,128)(2,1)} %amp_ref.1) | copy-start | bytes 2359300
  1.7 55.6 %copy-start.1 = (s32[768,8]{0,1:T(8,128)S(1)}, s32[768,8]{0,1:T(8,128)}, u32[]{:S(2)}) copy-start(s32[768,8]{0,1:T(8,128)} %param.6) | copy-start | bytes 73732
  46.2 11.1 %collective-permute-start = (bf16[1536,256]{1,0:T(8,128)(2,1)S(1)}, bf16[1536,256]{1,0:T(8,128)(2,1)S(1)}, u32[]{:S(2)}, u32[]{:S(2)}) collective-permute-start(bf16[1536,256]{1,0:T(8,128)(2,1)S(1)} %all_gather.9.own_ref), channel_id=1, source_target_pairs={{0,1},{1,0},{2,3},{3,2},{4,5},{5,4},{6,7},{7,6},{8,9},{9,8},{10,11... | collective-permute-start | bytes 2359304 | tf_op jit(solution)/shard_map/ppermute | solution.py:130
  75.6 21.6 %copy-start.2 = (f32[4,1024]{1,0:T(4,128)S(1)}, f32[4,1024]{1,0:T(4,128)}, u32[]{:S(2)}) copy-start(f32[4,1024]{1,0:T(4,128)} %param.7) | copy-start | bytes 49156

commit v9 on v7

--- a/solution.py
+++ b/solution.py
@@ -18,6 +18,7 @@
 SWAP = ((0, 1), (1, 0))
 CHIPS = 16
 RING = (0, *range(1, CHIPS, 2), *range(CHIPS - 2, 0, -2))
+SNAKE = tuple(4 * y + (x if y % 2 == 0 else 3 - x) for y in range(4) for x in range(4))
 WINDOW = 2 * TILE
 MIB = 1024 * 1024
 
@@ -81,11 +82,11 @@
     exponent = jnp.floor(jnp.log2(jnp.maximum(jnp.full((8, TILE), largest), 2.0**-100))) - 10.0
     scale = 0.5 * jnp.exp2(-exponent[:1, :1])
     places, rows = out_ref.shape[0], out_ref.shape[1] // 2
-    for place in range(places):
+    for slot, place in enumerate(SNAKE):
         for zh in range(2):
             piece = total[pl.ds((zh * places + place) * rows, rows), :]
-            out_ref[place, pl.ds(zh * rows, rows), :width] = piece * scale
-        out_ref[place, :, width:] = exponent
+            out_ref[slot, pl.ds(zh * rows, rows), :width] = piece * scale
+        out_ref[slot, :, width:] = exponent
 
 
 def combine_kernel(parts_ref, mine_ref, theirs_ref, zh_ref):
@@ -140,7 +141,7 @@
         compiler_params=pltpu.CompilerParams(vmem_limit_bytes=12 * MIB),
         name="ladder",
     )(mask, amplitudes, own, other)
-    parts = lax.all_to_all(ladder.astype(jnp.float16), PLANE, 0, 0, tiled=True)
+    parts = lax.all_to_all(ladder.astype(jnp.float16), PLANE, 0, 0, tiled=True, axis_index_groups=[SNAKE])
     mine, theirs, zh = pl.pallas_call(
         combine_kernel,
         out_shape=tuple(jax.ShapeDtypeStruct(residual_in.shape, t) for t in (jnp.float32, jnp.float32, jnp.int32)),

time: 98.2 us -> 97.6 us (level)
  blocking collectives: 84.8 us -> 83.6 us
    all_to_all x1, blocking collectives: 15.9 us -> 14.7 us  [per_device(): lax.all_to_all(ladder.astype(jnp.float16), PLANE, 0, 0, tiled=True, axis_...]
where the time goes in v9:
time: 97.6 us; the launch traced here: 95.9 us
  blocking collectives  83.6 us (86%)
  starting transfers between devices  5.55 us (6%)
  Pallas kernels  4.03 us (4%)
  waiting for transfers between devices  1.89 us (2%)
    all_gather x1, blocking collectives, per_device(): lax.all_gather(packed, INTEG, axis=0, tiled=True, axis_index_groups=rings)  47.3 us
    all_gather x1, blocking collectives, per_device(): both = lax.all_gather(theirs, 'zh', axis=0)  21.6 us
    all_to_all x1, blocking collectives, per_device(): lax.all_to_all(ladder.astype(jnp.float16), PLANE, 0, 0, tiled=True, axis_...  14.7 us
    ppermute x1, starting transfers between devices, per_device(): other = lax.ppermute(own, 'c', SWAP)  5.55 us
    pallas_call x1, Pallas kernels, per_device(): pl.pallas_call(functools.partial(ladder_kernel, tiles), out_shape=jax.Sha...  2.25 us
  transfers between devices with their start and end apart: 1, of which 1 were waited for; matrix products, arithmetic and copies ran while one was open for 0% of the time, Pallas kernels for 0%

profile of v9, /device:TPU:1, one launch (start us, length us, event | category | flops | bytes accessed | tf_op | source)
XLA Modules:
  0.0 95.9 jit_solution(5084379309431996575)
XLA Ops:
  0.0 0.0 copy-start
  0.0 1.7 %compress.1 = bf16[96,256]{1,0:T(8,128)(2,1)} custom-call(s32[8,768]{1,0:T(8,128)} %bitcast.14, bf16[96,1024]{1,0:T(8,128)(2,1)} %rows_hbm.1), custom_call_target="tpu_custom_call" | custom-call | tf_op jit(solution)/shard_map/compress/pallas_call | solution.py:113
  1.7 0.0 copy-start.1
  1.7 47.3 %all_gather.9.own_ref = bf16[1536,256]{1,0:T(8,128)(2,1)S(1)} all-gather(bf16[96,256]{1,0:T(8,128)(2,1)} %compress.1), channel_id=1, replica_groups={{0,2,6,10,14,18,22,26,30,28,24,20,16,12,8,4},{1,3,7,11,15,19,23,27,31,2..., dimensions={0}, use_global_device_ids=true | all-gather | bytes 835584 | tf_op jit(solution)/shard_map/all_gather | solution.py:128
  49.0 5.6 %collective-permute-start = (bf16[1536,256]{1,0:T(8,128)(2,1)S(1)}, bf16[1536,256]{1,0:T(8,128)(2,1)S(1)}, u32[]{:S(2)}, u32[]{:S(2)}) collective-permute-start(bf16[1536,256]{1,0:T(8,128)(2,1)S(1)} %all_gather.9.own_ref), channel_id=1, source_target_pairs={{0,1},{1,0},{2,3},{3,2},{4,5},{5,4},{6,7},{7,6},{8,9},{9,8},{10,11... | collective-permute-start | bytes 2359304 | tf_op jit(solution)/shard_map/ppermute | solution.py:129
  54.6 1.9 %collective-permute-done.other_ref = bf16[1536,256]{1,0:T(8,128)(2,1)S(1)} collective-permute-done((bf16[1536,256]{1,0:T(8,128)(2,1)S(1)}, bf16[1536,256]{1,0:T(8,128)(2,1)S(1)}, u32[]{:S(2)}, u32[]{:S(2)}) %collective-permute-start) | collective-permute-done | bytes 786464 | tf_op jit(solution)/shard_map/ppermute | solution.py:129
  56.4 0.0 copy-done
  56.4 0.0 copy-done.1
  56.4 2.3 %ladder.1 = f32[16,8,1152]{2,1,0:T(8,128)S(1)} custom-call(s32[8,768]{1,0:T(8,128)S(1)} %bitcast.15, bf16[128,3072]{1,0:T(8,128)(2,1)S(1)} %copy-done, bf16[1536,256]{1,0:T(8,128)(2,1)S(1)} %all_gather.9.own_ref, bf16[1536,256]{1,0:T(8,128)(2,1)S(1)} %collective-permute-done.other_ref), custom_call_target="tpu_custom_call" | custom-call | tf_op jit(solution)/shard_map/ladder/pallas_call | solution.py:130
  58.8 14.7 %all_to_all.5 = f16[16,8,1152]{2,1,0:T(8,128)(2,1)S(1)} all-to-all(f16[16,8,1152]{2,1,0:T(8,128)(2,1)S(1)} %convert_element_type.6), channel_id=1, replica_groups={{0,32,64,96,224,192,160,128,256,288,320,352,480,448,416,384},{1,33,65,9..., dimensions={0} | all-to-all | bytes 589824 | tf_op jit(solution)/shard_map/all_to_all | solution.py:144
  73.5 0.1 combine.1
  73.7 0.0 copy-start.2
  73.7 21.6 %all-gather.1 = f32[2,4,1024]{2,1,0:T(4,128)S(1)} all-gather(f32[1,4,1024]{2,1,0:T(4,128)S(1)} %bitcast.16), channel_id=2, replica_groups=mesh['zh'=2,'y'=4,'x'=4,'z'=16,'c'=2] {'zh'}, dimensions={0}, use_global_device_ids=true | all-gather | bytes 49152 | tf_op jit(solution)/shard_map/all_gather | solution.py:153
  95.3 0.0 copy-done.2
  95.3 0.6 fusion.2
  (2 shorter events, 0.1 us)
Async XLA Ops:
  0.0 56.4 %copy-start = (bf16[128,3072]{1,0:T(8,128)(2,1)S(1)}, bf16[128,3072]{1,0:T(8,128)(2,1)}, u32[]{:S(2)}) copy-start(bf16[128,3072]{1,0:T(8,128)(2,1)} %amp_ref.1) | copy-start | bytes 2359300
  1.7 54.8 %copy-start.1 = (s32[768,8]{0,1:T(8,128)S(1)}, s32[768,8]{0,1:T(8,128)}, u32[]{:S(2)}) copy-start(s32[768,8]{0,1:T(8,128)} %param.6) | copy-start | bytes 73732
  49.0 7.4 %collective-permute-start = (bf16[1536,256]{1,0:T(8,128)(2,1)S(1)}, bf16[1536,256]{1,0:T(8,128)(2,1)S(1)}, u32[]{:S(2)}, u32[]{:S(2)}) collective-permute-start(bf16[1536,256]{1,0:T(8,128)(2,1)S(1)} %all_gather.9.own_ref), channel_id=1, source_target_pairs={{0,1},{1,0},{2,3},{3,2},{4,5},{5,4},{6,7},{7,6},{8,9},{9,8},{10,11... | collective-permute-start | bytes 2359304 | tf_op jit(solution)/shard_map/ppermute | solution.py:129
  73.7 21.6 %copy-start.2 = (f32[4,1024]{1,0:T(4,128)S(1)}, f32[4,1024]{1,0:T(4,128)}, u32[]{:S(2)}) copy-start(f32[4,1024]{1,0:T(4,128)} %param.7) | copy-start | bytes 49156

commit v10 on v7

--- a/solution.py
+++ b/solution.py
@@ -59,15 +59,20 @@
             out_ref[rows, pl.ds(half * TILE, TILE)] = jnp.where(count > half, part, jnp.zeros_like(part))
 
 
-def ladder_kernel(tiles, mask_hbm, amp_ref, own_ref, other_ref, out_ref, mask, packed, total, mask_sem):
+def put_rows(which, rows_ref, packed):
+    for slot in range(CHIPS):
+        at = pl.multiple_of((2 * RING[slot] + which) * ROWS, GROUP)
+        packed[pl.ds(at, ROWS), :] = rows_ref[pl.ds(slot * ROWS, ROWS), :]
+
+
+def place_kernel(own_ref, packed):
+    put_rows(lax.axis_index("c"), own_ref, packed)
+
+
+def ladder_kernel(tiles, mask_hbm, amp_ref, placed_ref, other_ref, out_ref, packed, mask, total, mask_sem):
     mask_in, origin = mask_copy(mask_hbm, mask, mask_sem, tiles)
     mask_in.start()
-    core = lax.axis_index("c")
-    for slot in range(CHIPS):
-        rows = pl.ds(slot * ROWS, ROWS)
-        for which, ref in ((core, own_ref), (1 - core, other_ref)):
-            at = pl.multiple_of((2 * RING[slot] + which) * ROWS, GROUP)
-            packed[pl.ds(at, ROWS), :] = ref[rows, :]
+    put_rows(1 - lax.axis_index("c"), other_ref, packed)
     mask_in.wait()
     pairs, width = total.shape
     total[...] = jnp.zeros_like(total)
@@ -126,20 +131,30 @@
     rings = [[chip * cores + core for chip in RING] for core in range(cores)]
     own = lax.all_gather(packed, INTEG, axis=0, tiled=True, axis_index_groups=rings)
     other = lax.ppermute(own, "c", SWAP)
-    ladder = pl.pallas_call(
+    gathered = jax.ShapeDtypeStruct((2 * own.shape[0], own.shape[1]), own.dtype)
+    placed = pl.pallas_call(
+        place_kernel,
+        out_shape=gathered,
+        in_specs=[vmem_spec],
+        out_specs=vmem_spec,
+        compiler_params=pltpu.CompilerParams(vmem_limit_bytes=4 * MIB),
+        cost_estimate=pl.CostEstimate(flops=0, bytes_accessed=4 * own.size, transcendentals=0),
+        name="place",
+    )(own)
+    ladder, _ = pl.pallas_call(
         functools.partial(ladder_kernel, tiles),
-        out_shape=jax.ShapeDtypeStruct(messages, jnp.float32),
+        out_shape=(jax.ShapeDtypeStruct(messages, jnp.float32), gathered),
         in_specs=[hbm_spec] + [vmem_spec] * 3,
-        out_specs=vmem_spec,
+        out_specs=(vmem_spec, vmem_spec),
+        input_output_aliases={2: 1},
         scratch_shapes=[
             pltpu.SMEM((ab_tiles, WINDOW), jnp.int32),
-            pltpu.VMEM((32 * ROWS, 2 * TILE), jnp.bfloat16),
             pltpu.VMEM((pairs, width), jnp.float32),
             pltpu.SemaphoreType.DMA,
         ],
         compiler_params=pltpu.CompilerParams(vmem_limit_bytes=12 * MIB),
         name="ladder",
-    )(mask, amplitudes, own, other)
+    )(mask, amplitudes, placed, other)
     parts = lax.all_to_all(ladder.astype(jnp.float16), PLANE, 0, 0, tiled=True)
     mine, theirs, zh = pl.pallas_call(
         combine_kernel,

time: 98.2 us -> 98.3 us (level)
    pallas_call x1 -> x2, Pallas kernels: 2.25 us -> 2.25 us  [the longest x1 2.19 us: per_device(): pl.pallas_call(functools.partial(ladder_kernel, tiles), out_shape=(jax.Sh...]
where the time goes in v10:
time: 98.3 us; the launch traced here: 97.2 us
  blocking collectives  85 us (86%)
  starting transfers between devices  5.55 us (6%)
  Pallas kernels  4.04 us (4%)
  waiting for transfers between devices  1.82 us (2%)
    all_gather x1, blocking collectives, per_device(): lax.all_gather(packed, INTEG, axis=0, tiled=True, axis_index_groups=rings)  47.4 us
    all_gather x1, blocking collectives, per_device(): both = lax.all_gather(theirs, 'zh', axis=0)  21.6 us
    all_to_all x1, blocking collectives, per_device(): parts = lax.all_to_all(ladder.astype(jnp.float16), PLANE, 0, 0, tiled=True)  15.9 us
    ppermute x1, starting transfers between devices, per_device(): other = lax.ppermute(own, 'c', SWAP)  5.55 us
    pallas_call x1, Pallas kernels, per_device(): pl.pallas_call(functools.partial(ladder_kernel, tiles), out_shape=(jax.Sh...  2.19 us
  transfers between devices with their start and end apart: 1, of which 1 were waited for; matrix products, arithmetic and copies ran while one was open for 0% of the time, Pallas kernels for 0%

profile of v10, /device:TPU:1, one launch (start us, length us, event | category | flops | bytes accessed | tf_op | source)
XLA Modules:
  0.0 97.2 jit_solution(14714103230583479204)
XLA Ops:
  0.0 1.7 %compress.1 = bf16[96,256]{1,0:T(8,128)(2,1)} custom-call(s32[8,768]{1,0:T(8,128)} %bitcast.14, bf16[96,1024]{1,0:T(8,128)(2,1)} %rows_hbm.1), custom_call_target="tpu_custom_call" | custom-call | tf_op jit(solution)/shard_map/compress/pallas_call | solution.py:117
  1.7 0.0 copy-start
  1.7 0.0 copy-start.1
  1.7 47.4 %all_gather.9.own_ref = bf16[1536,256]{1,0:T(8,128)(2,1)S(1)} all-gather(bf16[96,256]{1,0:T(8,128)(2,1)} %compress.1), channel_id=1, replica_groups={{0,2,6,10,14,18,22,26,30,28,24,20,16,12,8,4},{1,3,7,11,15,19,23,27,31,2..., dimensions={0}, use_global_device_ids=true | all-gather | bytes 835584 | tf_op jit(solution)/shard_map/all_gather | solution.py:132
  49.1 5.6 %collective-permute-start = (bf16[1536,256]{1,0:T(8,128)(2,1)S(1)}, bf16[1536,256]{1,0:T(8,128)(2,1)S(1)}, u32[]{:S(2)}, u32[]{:S(2)}) collective-permute-start(bf16[1536,256]{1,0:T(8,128)(2,1)S(1)} %all_gather.9.own_ref), channel_id=1, source_target_pairs={{0,1},{1,0},{2,3},{3,2},{4,5},{5,4},{6,7},{7,6},{8,9},{9,8},{10,11... | collective-permute-start | bytes 2359304 | tf_op jit(solution)/shard_map/ppermute | solution.py:133
  54.7 0.1 place.1.placed_ref
  54.8 1.8 %collective-permute-done.other_ref = bf16[1536,256]{1,0:T(8,128)(2,1)S(1)} collective-permute-done((bf16[1536,256]{1,0:T(8,128)(2,1)S(1)}, bf16[1536,256]{1,0:T(8,128)(2,1)S(1)}, u32[]{:S(2)}, u32[]{:S(2)}) %collective-permute-start) | collective-permute-done | bytes 786464 | tf_op jit(solution)/shard_map/ppermute | solution.py:133
  56.6 0.0 copy-done
  56.6 0.0 copy-done.1
  56.6 2.2 %ladder.1 = (f32[16,8,1152]{2,1,0:T(8,128)S(1)}, bf16[3072,256]{1,0:T(8,128)(2,1)S(1)}) custom-call(s32[8,768]{1,0:T(8,128)S(1)} %bitcast.15, bf16[128,3072]{1,0:T(8,128)(2,1)S(1)} %copy-done, bf16[3072,256]{1,0:T(8,128)(2,1)S(1)} %place.1.placed_ref, bf16[1536,256]{1,0:T(8,128)(2,1)S(1)} %collective-permute-done.other_ref), custom_call_target="tpu_custom_call", output_to_operand_aliasing={{1}: (2, {})} | custom-call | tf_op jit(solution)/shard_map/ladder/pallas_call | solution.py:144
  58.8 0.0 copy-start.2
  58.8 15.9 %all_to_all.5 = f16[16,8,1152]{2,1,0:T(8,128)(2,1)S(1)} all-to-all(f16[16,8,1152]{2,1,0:T(8,128)(2,1)S(1)} %convert_element_type.6), channel_id=1, replica_groups=mesh['zh'=2,'y'=4,'x'=4,'z'=16,'c'=2] {'y','x'}, dimensions={0} | all-to-all | bytes 589824 | tf_op jit(solution)/shard_map/all_to_all | solution.py:158
  74.8 0.1 combine.1
  74.9 21.6 %all-gather.1 = f32[2,4,1024]{2,1,0:T(4,128)S(1)} all-gather(f32[1,4,1024]{2,1,0:T(4,128)S(1)} %bitcast.16), channel_id=2, replica_groups=mesh['zh'=2,'y'=4,'x'=4,'z'=16,'c'=2] {'zh'}, dimensions={0}, use_global_device_ids=true | all-gather | bytes 49152 | tf_op jit(solution)/shard_map/all_gather | solution.py:167
  96.6 0.0 copy-done.2
  96.6 0.6 fusion.2
  (2 shorter events, 0.1 us)
Async XLA Ops:
  1.7 54.9 %copy-start = (bf16[128,3072]{1,0:T(8,128)(2,1)S(1)}, bf16[128,3072]{1,0:T(8,128)(2,1)}, u32[]{:S(2)}) copy-start(bf16[128,3072]{1,0:T(8,128)(2,1)} %amp_ref.1) | copy-start | bytes 2359300
  1.7 54.9 %copy-start.1 = (s32[768,8]{0,1:T(8,128)S(1)}, s32[768,8]{0,1:T(8,128)}, u32[]{:S(2)}) copy-start(s32[768,8]{0,1:T(8,128)} %param.6) | copy-start | bytes 73732
  49.1 7.4 %collective-permute-start = (bf16[1536,256]{1,0:T(8,128)(2,1)S(1)}, bf16[1536,256]{1,0:T(8,128)(2,1)S(1)}, u32[]{:S(2)}, u32[]{:S(2)}) collective-permute-start(bf16[1536,256]{1,0:T(8,128)(2,1)S(1)} %all_gather.9.own_ref), channel_id=1, source_target_pairs={{0,1},{1,0},{2,3},{3,2},{4,5},{5,4},{6,7},{7,6},{8,9},{9,8},{10,11... | collective-permute-start | bytes 2359304 | tf_op jit(solution)/shard_map/ppermute | solution.py:133
  58.8 37.8 %copy-start.2 = (f32[4,1024]{1,0:T(4,128)S(1)}, f32[4,1024]{1,0:T(4,128)}, u32[]{:S(2)}) copy-start(f32[4,1024]{1,0:T(4,128)} %param.7) | copy-start | bytes 49156
